TPU v7x, 32 devices: a whole 2x2x4 slice. The times are simulated.
32 devices in a mesh: gx: 4 (over x, core), gz: 8 (over z, y).
Axes of the slice: x: 2, y: 2, z: 4, core: 2. Of those that a mesh axis runs over, the one named last changes fastest.
Arguments:
- velocity: float32 [3, 2048, 8, 2048], P(None, 'gx', None, 'gz'), may hold values from -32 to 32
Outputs:
- grad_x: float32 [3, 2048, 8, 2048], P(None, 'gx', None, 'gz')
- grad_z: float32 [3, 2048, 8, 2048], P(None, 'gx', None, 'gz')
- convect: float32 [3, 2048, 8, 2048], P(None, 'gx', None, 'gz')
- rebuilt: float32 [2, 2048, 8, 2048], P(None, 'gx', None, 'gz')
All inputs are finite; a program needn't handle non-finite values.
Results may differ from a plain program's by a relative error of at most 0.0003.
Values sent between devices are 32-bit elements; how exact they have to be, the bound alone decides.
A program may use at most 256 MiB of HBM per device.

v0:
```python
import math

import jax
import jax.numpy as jnp
from jax import lax
from jax.sharding import PartitionSpec as P

ALPHA = 1.0 / 3.0
COEF_A = 14.0 / 9.0
COEF_B = 1.0 / 9.0
BLOCK_CAP = 128


def with_halo(array, sides, width):
    for axis, dim in sides:
        peers, length = (lax.axis_size(axis), array.shape[dim])
        up = [(i, (i + 1) % peers) for i in range(peers)]
        down = [(j, i) for i, j in up]
        last = lax.slice_in_dim(array, length - width, length, axis=dim)
        initial = lax.slice_in_dim(array, 0, width, axis=dim)
        before = lax.ppermute(last, axis, up)
        after = lax.ppermute(initial, axis, down)
        array = jnp.concatenate([before, array, after], axis=dim)
    return array


def entering(array, axis, combine, identity):
    peers, mine = (lax.axis_size(axis), lax.axis_index(axis))
    everything = lax.all_gather(array, axis)
    start = jnp.broadcast_to(jnp.asarray(identity, array.dtype), array.shape)

    def hop(k, before):
        reached = k < mine
        new = combine(before, everything[k])
        return jnp.where(reached, new, before)

    return lax.fori_loop(0, peers, hop, start)


def matmul_high(left_matrix, right_matrix):
    return jnp.dot(left_matrix, right_matrix, precision=lax.Precision.HIGHEST)


def block_inverse(length):
    offsets = jnp.arange(length)
    neighbour = (jnp.abs(offsets[:, None] - offsets[None, :]) == 1).astype(jnp.float32) * ALPHA
    identity = jnp.eye(length, dtype=jnp.float32)
    inverse = identity - neighbour
    near_power = neighbour
    for squaring in range(7):
        near_power = matmul_high(near_power, near_power)
        inverse = matmul_high(inverse, identity + near_power)
    return inverse


def explicit(padded, axis_at, length):

    def cell_slice(offset):
        return lax.slice_in_dim(padded, offset, offset + length, axis=axis_at)

    return 0.5 * COEF_A * (cell_slice(3) - cell_slice(1)) + 0.25 * COEF_B * (
        cell_slice(4) - cell_slice(0)
    )


def apply_matrix(source, matrix, axis_at):
    shape_now = source.shape
    if axis_at == source.ndim - 1:
        return jnp.dot(source, matrix.T, precision=lax.Precision.HIGHEST)
    length = shape_now[axis_at]
    leading = math.prod(shape_now[:axis_at])
    trailing = math.prod(shape_now[axis_at + 1 :])
    flat = source.reshape(leading, length, trailing)
    batched = jnp.broadcast_to(matrix, (leading,) + matrix.shape)
    result = lax.dot_general(
        batched, flat, (((2,), (1,)), ((0,), (0,))), precision=lax.Precision.HIGHEST
    )
    return result.reshape(shape_now)


def blocked(values, axis_at, block):
    shape_now = values.shape
    return values.reshape(
        shape_now[:axis_at] + (shape_now[axis_at] // block, block) + shape_now[axis_at + 1 :]
    )


def correct(solved, inverse, axis_at, prev_last, next_first):
    length = solved.shape[axis_at]
    first_cell = lax.slice_in_dim(solved, 0, 1, axis=axis_at)
    last_cell = lax.slice_in_dim(solved, length - 1, length, axis=axis_at)
    pivot_term = ALPHA * inverse[0, 0]
    denom_pair = 1.0 - pivot_term * pivot_term
    left_value = (prev_last - pivot_term * first_cell) / denom_pair
    right_value = (next_first - pivot_term * last_cell) / denom_pair
    shape_list = [1] * solved.ndim
    shape_list[axis_at] = length
    left_column = inverse[:, 0].reshape(shape_list)
    right_column = inverse[:, length - 1].reshape(shape_list)
    return solved - ALPHA * (left_value * left_column + right_value * right_column)


def couple(solved, inverse, axis_at, edge_before, edge_after):
    block = solved.shape[axis_at + 1]
    count = solved.shape[axis_at]
    first_cells = lax.slice_in_dim(solved, 0, 1, axis=axis_at + 1)
    last_cells = lax.slice_in_dim(solved, block - 1, block, axis=axis_at + 1)
    prev_last = jnp.concatenate(
        [edge_before, lax.slice_in_dim(last_cells, 0, count - 1, axis=axis_at)], axis_at
    )
    next_first = jnp.concatenate(
        [lax.slice_in_dim(first_cells, 1, count, axis=axis_at), edge_after], axis_at
    )
    return correct(solved, inverse, axis_at + 1, prev_last, next_first)


def whole_lines(lines, axis_at, inverse):
    total = lines.shape[axis_at]
    block = inverse.shape[0]
    head_cells = lax.slice_in_dim(lines, total - 2, total, axis=axis_at)
    tail_cells = lax.slice_in_dim(lines, 0, 2, axis=axis_at)
    padded = jnp.concatenate([head_cells, lines, tail_cells], axis_at)
    source = explicit(padded, axis_at, total)
    solved = apply_matrix(blocked(source, axis_at, block), inverse, axis_at + 1)
    count = solved.shape[axis_at]
    last_cells = lax.slice_in_dim(solved, block - 1, block, axis=axis_at + 1)
    first_cells = lax.slice_in_dim(solved, 0, 1, axis=axis_at + 1)
    edge_before = lax.slice_in_dim(last_cells, count - 1, count, axis=axis_at)
    edge_after = lax.slice_in_dim(first_cells, 0, 1, axis=axis_at)
    return couple(solved, inverse, axis_at, edge_before, edge_after).reshape(lines.shape)


def running_sum(values, axis_at):
    length = values.shape[axis_at]
    offsets = jnp.arange(length)
    lower = (offsets[:, None] > offsets[None, :]).astype(jnp.float32)
    return apply_matrix(values, lower, axis_at)


def line_terms(values, axis_at, start, total_len):
    length = values.shape[axis_at]
    shape_list = [1] * values.ndim
    shape_list[axis_at] = length
    position = (start + jnp.arange(length)).astype(jnp.float32).reshape(shape_list)
    centred = position - 0.5 * (total_len - 1)
    return (jnp.sum(values, axis_at), jnp.sum(values * centred, axis_at), position)


def primitive(values, axis_at, position, before_sum, total_sum, centred_sum, total_len):
    mean_value = jnp.expand_dims(total_sum, axis_at) / total_len
    inside = running_sum(values, axis_at) + jnp.expand_dims(before_sum, axis_at)
    result = inside - position * mean_value + 0.5 * (values - mean_value)
    result = result + jnp.expand_dims(centred_sum, axis_at) / total_len
    return -result / math.sqrt(total_len)


def add_terms(earlier, later):
    return earlier + later


def body(velocity):
    cells_x = velocity.shape[1]
    cells_z = velocity.shape[3]
    total_x = cells_x * lax.axis_size("gx")
    total_z = cells_z * lax.axis_size("gz")
    block_x = min(cells_x, BLOCK_CAP)
    inverse_x = block_inverse(block_x)
    fields_x = jnp.concatenate([velocity, velocity[0][None] * velocity], 0)
    fields_z = jnp.concatenate([velocity, velocity[2][None] * velocity], 0)
    padded_x = with_halo(fields_x, (("gx", 1),), 2)
    solved_x = apply_matrix(blocked(explicit(padded_x, 1, cells_x), 1, block_x), inverse_x, 2)
    rimmed_x = with_halo(solved_x.reshape(fields_x.shape), (("gx", 1),), 1)
    edge_before_x = rimmed_x[:, 0:1][:, :, None]
    edge_after_x = rimmed_x[:, cells_x + 1 : cells_x + 2][:, :, None]
    deriv_x = couple(solved_x, inverse_x, 1, edge_before_x, edge_after_x).reshape(fields_x.shape)
    solved_lines_z = whole_lines(
        lax.all_to_all(fields_z, "gz", split_axis=1, concat_axis=3, tiled=True), 3, inverse_x
    )
    deriv_z = lax.all_to_all(solved_lines_z, "gz", split_axis=3, concat_axis=1, tiled=True)
    slope_u = deriv_x[0]
    slope_w = deriv_z[2]
    sum_z, moment_z, position_z = line_terms(slope_u, 2, lax.axis_index("gz") * cells_z, total_z)
    sum_x, moment_x, position_x = line_terms(slope_w, 0, lax.axis_index("gx") * cells_x, total_x)
    before_z = entering(sum_z, "gz", add_terms, jnp.zeros_like(sum_z))
    line_sum_z, centred_z = lax.psum((sum_z, moment_z), "gz")
    before_x = entering(sum_x, "gx", add_terms, jnp.zeros_like(sum_x))
    line_sum_x, centred_x = lax.psum((sum_x, moment_x), "gx")
    rebuilt_x = primitive(slope_w, 0, position_x, before_x, line_sum_x, centred_x, total_x)
    rebuilt_z = primitive(slope_u, 2, position_z, before_z, line_sum_z, centred_z, total_z)
    grad_x = deriv_x[0:3]
    grad_z = deriv_z[0:3]
    convect = deriv_x[3:6] + deriv_z[3:6]
    rebuilt = jnp.stack([rebuilt_x, rebuilt_z])
    return (grad_x, grad_z, convect, rebuilt)


def solution(mesh):
    placed = (P(None, "gx", None, "gz"),)
    return jax.shard_map(
        body,
        mesh=mesh,
        in_specs=placed,
        out_specs=(
            P(None, "gx", None, "gz"),
            P(None, "gx", None, "gz"),
            P(None, "gx", None, "gz"),
            P(None, "gx", None, "gz"),
        ),
        check_vma=False,
    )
```

profile of v0, /device:TPU:0, one launch (start us, length us, event | category | flops | bytes accessed | tf_op | source)
XLA Modules:
  0.0 1901.8 jit_solution(15984450574781134631)
XLA Ops:
  0.6 6.3 slice_bitcast_fusion
  9.2 9.4 fusion.57
  18.6 17.3 pad_maximum_fusion.3
  35.8 7.5 all-to-all-start
  49.0 538.4 %all-to-all-done = f32[6,512,8,256]{3,2,0,1:T(8,128)} async-done(((f32[6,512,8,256]{3,2,0,1:T(8,128)}), f32[6,512,8,256]{3,2,0,1:T(8,128)}, u32[]{:S(2)}, u32[]{:S(2)}) %all-to-all-start) | async-done | bytes 25165856 | tf_op jit(solution)/shard_map/all_to_all | solution.py:177
  587.4 24.7 %copy.170 = f32[6,8,64,8,256]{4,1,3,2,0:T(8,128)} copy(f32[6,8,64,8,256]{4,3,0,2,1:T(8,128)} %bitcast.11) | data formatting | bytes 50331648 | tf_op jit(solution)/shard_map/all_to_all | solution.py:177
  612.1 26.8 %all_to_all.27 = f32[6,64,8,2048]{3,2,1,0:T(8,128)} reshape(f32[6,64,8,8,256]{4,3,2,1,0:T(8,128)} %bitcast.117) | data formatting | bytes 50331648 | tf_op jit(solution)/shard_map/all_to_all | solution.py:177
  641.3 54.3 %fusion.4 = f32[6,64,8,16,128]{4,2,3,1,0:T(8,128)} fusion(f32[6,64,8,2]{3,2,1,0:T(8,128)S(1)} %get-tuple-element.259, f32[6,64,8,2048]{3,2,1,0:T(8,128)} %all_to_all.27, f32[6,64,8,2]{3,2,1,0:T(8,128)S(1)} %get-tuple-element.258), kind=kLoop, calls=%fused_computation.12 | loop fusion | flops 56623104 | bytes 50380800 | tf_op jit(solution)/shard_map/reshape | solution.py:83
  695.6 28.7 %fusion.11 = f32[6,64,8,16,128]{4,3,2,1,0:T(8,128)} fusion(f32[6,64,8,16,128]{4,2,3,1,0:T(8,128)} %fusion.4, f32[128,128]{0,1:T(8,128)S(1)} %fusion.63), kind=kOutput, calls=%fused_computation.24 | convolution fusion | flops 9663676416 | bytes 50397184 | tf_op jit(solution)/shard_map/dot_general | solution.py:69
  724.3 35.1 %fusion.54 = (f32[6,64,8,15,1]{4,3,2,1,0:T(8,128)}, f32[6,64,8,15,1]{4,3,2,1,0:T(8,128)}) fusion(f32[6,64,8,16,128]{4,3,2,1,0:T(8,128)} %fusion.11), kind=kLoop, calls=%fused_computation.109 | loop fusion | bytes 737280 | tf_op jit(solution)/shard_map/slice | solution.py:109
  759.4 35.2 %fusion.52 = (f32[6,64,8,16,1]{4,3,2,1,0:T(8,128)}, f32[6,64,8,16,1]{4,3,2,1,0:T(8,128)}) fusion(f32[6,64,8,16,128]{4,3,2,1,0:T(8,128)} %fusion.11), kind=kLoop, calls=%fused_computation.107 | loop fusion | bytes 786432 | tf_op jit(solution)/shard_map/slice | solution.py:90
  794.5 9.9 fusion.53
  804.5 18.1 copy.134
  822.6 18.1 copy.137
  840.6 18.1 copy.160
  858.7 18.5 copy.161
  883.3 18.2 multiply_subtract_fusion
  901.5 31.8 %copy.156 = f32[6,64,8,16,128]{1,2,0,4,3:T(8,128)} copy(f32[6,64,8,16,128]{4,3,2,1,0:T(8,128)} %multiply_subtract_fusion) | data formatting | bytes 50331648 | tf_op jit(solution)/shard_map/reshape | solution.py:130
  933.3 66.9 %reshape.123 = f32[8,1,786432]{2,1,0:T(1,128)} reshape(f32[2048,6,8,64]{3,2,1,0:T(8,128)} %bitcast.108) | data formatting | bytes 50331648
  1000.2 6.4 all-to-all-start.1
  1006.7 11.7 broadcast_multiply_fusion.1
  1023.8 31.8 %pad_maximum_fusion = (f32[6,514,8,256]{3,2,1,0:T(8,128)}, f32[6,514,8,256]{3,2,1,0:T(8,128)}) fusion(f32[6,2,8,256]{3,2,1,0:T(8,128)S(1)} %collective-permute-done, f32[3,512,8,256]{3,2,1,0:T(8,128)} %broadcast_multiply_fusion.1, f32[3,512,8,256]{3,2,1,0:T(8,128)} %param.5, f32[6,2,8,256]{3,2,1,0:T(8,128)S(1)} %collective-permute-done.1), kind=kLoop, calls=%fused_computation.6 | loop fusion | flops 25264128 | bytes 75890688 | tf_op jit(solution)/shard_map/concatenate | solution.py:23
  1055.6 40.5 %fusion.9 = f32[6,512,8,256]{3,2,1,0:T(8,128)} fusion(f32[6,514,8,256]{3,2,1,0:T(8,128)} %get-tuple-element.267, f32[6,514,8,256]{3,2,1,0:T(8,128)} %get-tuple-element.266), kind=kLoop, calls=%fused_computation.20 | loop fusion | flops 31457280 | bytes 125829120 | tf_op jit(solution)/shard_map/add | solution.py:61
  1096.1 26.8 %reshape_reshape.6 = f32[24,128,2048]{2,1,0:T(8,128)} reshape(f32[6,512,8,256]{3,2,1,0:T(8,128)} %fusion.9) | data formatting | bytes 50331648 | tf_op jit(solution)/shard_map/reshape;reshape | solution.py:73
  1122.9 29.1 %fusion.15 = f32[24,128,2048]{2,1,0:T(8,128)} fusion(f32[24,128,2048]{2,1,0:T(8,128)} %reshape_reshape.6, f32[128,128]{1,0:T(8,128)S(1)} %copy.125), kind=kOutput, calls=%fused_computation.41 | convolution fusion | flops 9663676416 | bytes 50397184 | tf_op jit(solution)/shard_map/dot_general | solution.py:75
  1152.0 15.7 copy.162
  1171.3 4.6 copy-done.2
  1176.0 10.9 multiply_subtract_fusion.1
  1186.9 8.3 copy-done.1
  1198.0 5.6 copy.149
  1203.6 368.5 %all-reduce = (f32[512,8]{0,1:T(8,128)S(1)}, f32[512,8]{0,1:T(8,128)S(1)}) all-reduce(f32[512,8]{0,1:T(8,128)S(1)} %copy.152, f32[512,8]{0,1:T(8,128)S(1)} %copy.151), channel_id=1, replica_groups=mesh['gx'=4,'gz'=8] {'gz'}, use_global_device_ids=true, to_apply=%region_11.12 | all-reduce | flops 8192 | bytes 65536 | tf_op jit(solution)/shard_map/psum | solution.py:185
  1572.1 30.5 %all_gather.15 = f32[8,512,8]{1,2,0:T(8,128)S(1)} all-gather(f32[1,512,8]{1,2,0:T(8,128)S(1)} %copy.150), channel_id=1, replica_groups=mesh['gx'=4,'gz'=8] {'gz'}, dimensions={0}, use_global_device_ids=true | all-gather | bytes 147456 | tf_op jit(solution)/shard_map/all_gather | solution.py:29
  1602.9 6.6 multiply_bitcast_fusion
  1609.5 18.1 fusion.51
  1628.2 71.2 %reduce.4 = f32[8,786432]{1,0:T(8,128)} reduce(f32[8,1,786432]{2,1,0:T(1,128)} %all-to-all-done.1, f32[]{:T(128)} %broadcast.110), dimensions={1}, to_apply=%all_to_all.28.reduce_sub_computation | reduce | bytes 50331652 | tf_op jit(solution)/shard_map/all_to_all | solution.py:179
  1699.5 52.5 %reshape.124 = f32[2048,6,8,64]{3,2,1,0:T(8,128)} reshape(f32[8,786432]{1,0:T(8,128)} %reduce.4) | data formatting | bytes 50331648
  1752.0 33.7 %copy.157 = f32[6,64,8,8,256]{4,3,2,1,0:T(8,128)} copy(f32[6,64,8,8,256]{1,2,0,4,3:T(8,128)} %bitcast.109) | data formatting | bytes 50331648 | tf_op jit(solution)/shard_map/all_to_all | solution.py:179
  1791.7 4.4 copy.147
  1796.1 18.5 fusion.50
  1814.5 5.2 all-gather
  1819.7 10.5 all-reduce.1
  1830.2 6.1 copy.164
  1836.4 5.4 copy.146
  1841.9 8.5 multiply_bitcast_fusion.1
  1853.2 8.3 copy.153
  1861.4 12.8 copy.144
  1874.3 13.1 copy.143
  1887.4 14.0 add.192
  (90 shorter events, 36.0 us)
Async XLA Ops:
  0.6 8.5 copy-start
  35.8 551.6 %all-to-all-start = ((f32[6,512,8,256]{3,2,0,1:T(8,128)}), f32[6,512,8,256]{3,2,0,1:T(8,128)}, u32[]{:S(2)}, u32[]{:S(2)}) async-start(f32[6,512,8,256]{3,2,0,1:T(8,128)} %pad_maximum_fusion.3), calls=%async_computation | async-start | bytes 50331648 | tf_op jit(solution)/shard_map/all_to_all | solution.py:177
  46.5 649.1 %copy-start.3 = (f32[128,128]{0,1:T(8,128)}, f32[128,128]{0,1:T(8,128)S(1)}, u32[]{:S(2)}) copy-start(f32[128,128]{0,1:T(8,128)S(1)} %fusion.63) | copy-start | bytes 196612
  48.9 834.3 %copy-start.7 = (f32[128]{0:T(128)}, f32[128]{0:T(128)S(1)}, u32[]{:S(2)}) copy-start(f32[128]{0:T(128)S(1)} %get-tuple-element.274) | copy-start | bytes 1540
  48.9 834.3 %copy-start.9 = (f32[128]{0:T(128)}, f32[128]{0:T(128)S(1)}, u32[]{:S(2)}) copy-start(f32[128]{0:T(128)S(1)} %get-tuple-element.275) | copy-start | bytes 1540
  1000.2 627.4 %all-to-all-start.1 = ((f32[8,1,786432]{2,1,0:T(1,128)}), f32[8,1,786432]{2,1,0:T(1,128)}, u32[]{:S(2)}, u32[]{:S(2)}) async-start(f32[8,1,786432]{2,1,0:T(1,128)} %reshape.123), calls=%async_computation.1 | async-start | bytes 50331648 | tf_op jit(solution)/shard_map/all_to_all | solution.py:179
  1006.7 13.1 copy-start.4
  1019.2 3.0 collective-permute-start
  1019.3 4.5 collective-permute-start.1
  1152.0 24.0 %copy-start.8 = (f32[128]{0:T(128)S(1)}, f32[128]{0:T(128)}, u32[]{:S(2)}) copy-start(f32[128]{0:T(128)} %copy-done.7) | copy-start | bytes 1540
  1152.0 24.0 %copy-start.10 = (f32[128]{0:T(128)S(1)}, f32[128]{0:T(128)}, u32[]{:S(2)}) copy-start(f32[128]{0:T(128)} %copy-done.9) | copy-start | bytes 1540
  1167.6 8.3 copy-start.2
  1167.7 3.6 collective-permute-start.2
  1167.7 3.5 collective-permute-start.3
  1186.8 8.3 copy-start.1
  1751.9 33.7 %copy-start.6 = (f32[8,64]{0,1:T(8,128)S(1)}, f32[8,64]{0,1:T(8,128)}, u32[]{:S(2)}) copy-start(f32[8,64]{0,1:T(8,128)} %copy.148) | copy-start | bytes 6148
  1796.0 45.7 %copy-start.5 = (f32[8,256]{1,0:T(8,128)S(1)}, f32[8,256]{1,0:T(8,128)}, u32[]{:S(2)}) copy-start(f32[8,256]{1,0:T(8,128)} %custom-call) | copy-start | bytes 24580
  1796.0 45.8 %copy-start.11 = (f32[512]{0:T(512)S(1)}, f32[512]{0:T(512)}, u32[]{:S(2)}) copy-start(f32[512]{0:T(512)} %add_convert_fusion) | copy-start | bytes 6148
where the time goes:
time: 1910 us; the launch traced here: 1900 us
  local copies, waits for them, and re-layouts  558 us (29%)
  waiting for transfers between devices  543 us (28%)
  blocking collectives  415 us (22%)
  other arithmetic  291 us (15%)
  matrix products  75.8 us (4%)
    all_to_all x1, waiting for transfers between devices, body(): lax.all_to_all(fields_z, 'gz', split_axis=1, concat_axis=3, tiled=True)  538 us
    psum x1, blocking collectives, body(): line_sum_z, centred_z = lax.psum((sum_z, moment_z), 'gz')  368 us
    unnamed x32, local copies, waits for them, and re-layouts  201 us
    all_to_all x1, other arithmetic, body(): lax.all_to_all(solved_lines_z, 'gz', split_axis=3, concat_axis=1, tiled=T...  71.2 us
    reshape x1, other arithmetic, blocked(): values.reshape(shape_now[:axis_at] + (shape_now[axis_at] // block, block)...  54.3 us
    slice x3, local copies, waits for them, and re-layouts, couple(): lax.slice_in_dim(last_cells, 0, count - 1, axis=axis_at)  53.2 us
    all_to_all x2, local copies, waits for them, and re-layouts, body(): lax.all_to_all(fields_z, 'gz', split_axis=1, concat_axis=3, tiled=True)  51.5 us
    slice x3, local copies, waits for them, and re-layouts, body(): convect = deriv_x[3:6] + deriv_z[3:6]  49.5 us
  transfers between devices with their start and end apart: 6, of which 4 were waited for; matrix products, arithmetic and copies ran while one was open for 11% of the time, Pallas kernels for 0%

commit v1 on v0

v1 whole, which is shorter than its diff:
```python
import functools
import math

import jax
import jax.numpy as jnp
import ml_dtypes
import numpy as np
from jax import lax
from jax.experimental import pallas as pl
from jax.experimental.pallas import tpu as pltpu
from jax.sharding import PartitionSpec as P

ROOT = (math.sqrt(5.0) - 3.0) / 2.0
C = 25.0 / 12.0
KAPPA = -1.0 / 12.0
TX = 64
STEP = 4
F32 = jnp.float32
BF16 = jnp.bfloat16
LIMIT = 52 * 1024 * 1024
MESH = pl.DeviceIdType.MESH


def halves(array):
    high = array.astype(ml_dtypes.bfloat16)
    low = (array - high.astype(np.float64)).astype(ml_dtypes.bfloat16)
    return high, low


def split(value):
    high = value.astype(BF16)
    low = (value - high.astype(F32)).astype(BF16)
    return high, low


def mm(left, right):
    return jnp.dot(left, right, preferred_element_type=F32)


def kernel_values(offset):
    size = np.abs(offset)
    power = np.power(np.abs(ROOT), size) * np.where(size % 2 == 0, 1.0, -1.0)
    value = np.sign(offset) * C * power
    return value + np.where(size == 1, np.sign(offset) * KAPPA, 0.0)


def signed_power(exponent):
    return np.power(np.abs(ROOT), exponent) * np.where(exponent % 2 == 0, 1.0, -1.0)


def derivative_matrices(cz):
    at = np.arange(cz)
    return halves(kernel_values(at[None, :] - at[:, None]))


def edge_weights(cz):
    at = np.arange(cz)
    out = np.zeros((6, cz, 128))
    low_out = np.zeros((6, cz, 128))
    for f in range(6):
        base = np.zeros((cz, 32))
        base[:, f] = signed_power(cz - at)
        base[cz - 1, 6 + f] = 1.0
        base[:, 16 + f] = signed_power(at + 1)
        base[0, 22 + f] = 1.0
        high, low = halves(base)
        out[f, :, 0:32] = high.astype(np.float64)
        out[f, :, 32:64] = low.astype(np.float64)
        low_out[f, :, 0:32] = high.astype(np.float64)
    return out.astype(ml_dtypes.bfloat16), low_out.astype(ml_dtypes.bfloat16)


def correction_matrices(cz):
    at = np.arange(cz)
    out = np.zeros((6, 128, cz))
    for f in range(6):
        base = np.zeros((32, cz))
        base[f] = C * signed_power(at)
        base[6 + f, 0] = KAPPA
        base[16 + f] = -C * signed_power(cz - 1 - at)
        base[22 + f, cz - 1] = -KAPPA
        high, low = halves(base)
        out[f, 0:32] = high.astype(np.float64)
        out[f, 32:64] = high.astype(np.float64)
        out[f, 64:96] = low.astype(np.float64)
    return out.astype(ml_dtypes.bfloat16)


def fields(planes, pivot):
    return list(planes) + [planes[pivot] * p for p in planes]


def edges_kernel(steps, v_ref, wa_ref, wb_ref, ck_ref, xup_ref, xdn_ref, zup_ref, zdn_ref, back, fore):
    s = pl.program_id(0)
    cz = v_ref.shape[3]
    rows = TX * 8

    @pl.when(s == 0)
    def _():
        back[...] = jnp.zeros_like(back)
        fore[...] = jnp.zeros_like(fore)
        xup_ref[6:9] = v_ref[:, TX - 1]

    ck_ref[0] = back[...]

    def sweep(k, state):
        states = list(state)
        for j in range(STEP):
            i = TX - 1 - (k * STEP + j)
            now = fields([v_ref[c, i] for c in range(3)], 0)
            states = [ROOT * (f + b) for f, b in zip(now, states)]
        return tuple(states)

    final = lax.fori_loop(0, TX // STEP, sweep, tuple(back[c] for c in range(6)))
    for c in range(6):
        back[c] = final[c]
    back[6:9] = v_ref[:, 0]

    @pl.when(s * TX < 128)
    def _():
        def ahead(k, state):
            states = list(state)
            for j in range(STEP):
                i = k * STEP + j
                now = fields([v_ref[c, i] for c in range(3)], 0)
                states = [ROOT * (f + b) for f, b in zip(now, states)]
            return tuple(states)

        zero = jnp.zeros((8, cz), F32)
        ended = lax.fori_loop(0, TX // STEP, ahead, (zero,) * 6)
        scale = jnp.where(s == 0, F32(1.0), F32(ROOT**TX))
        for c in range(6):
            fore[c] = fore[c] + scale * ended[c]

    planes = [v_ref[c].reshape(rows, cz) for c in range(3)]
    total = jnp.zeros((rows, 128), F32)
    for f in range(6):
        value = planes[f] if f < 3 else planes[2] * planes[f - 3]
        high, low = split(value)
        total = total + mm(high, wa_ref[f]) + mm(low, wb_ref[f])
    turned = total.T
    message = turned[0:32] + turned[32:64]
    zup_ref[...] = message[0:16]
    zdn_ref[...] = message[16:32]

    @pl.when(s == steps - 1)
    def _():
        xup_ref[0:6] = fore[...]
        xdn_ref[...] = back[...]


def find_edges(velocity):
    _, cx, ny, cz = velocity.shape
    steps = cx // TX
    rows = TX * 8
    wa, wb = edge_weights(cz)
    whole = lambda shape: pl.BlockSpec(shape, lambda s: (0,) * len(shape))
    turned = lambda s: (0, steps - 1 - s)
    return pl.pallas_call(
        functools.partial(edges_kernel, steps),
        grid=(steps,),
        in_specs=[
            pl.BlockSpec((3, TX, 8, cz), lambda s: (0, steps - 1 - s, 0, 0)),
            whole((6, cz, 128)),
            whole((6, cz, 128)),
        ],
        out_specs=[
            pl.BlockSpec((1, 9, 8, cz), lambda s: (steps - 1 - s, 0, 0, 0)),
            whole((9, 8, cz)),
            whole((9, 8, cz)),
            pl.BlockSpec((16, rows), turned),
            pl.BlockSpec((16, rows), turned),
        ],
        out_shape=[
            jax.ShapeDtypeStruct((steps, 9, 8, cz), F32),
            jax.ShapeDtypeStruct((9, 8, cz), F32),
            jax.ShapeDtypeStruct((9, 8, cz), F32),
            jax.ShapeDtypeStruct((16, cx * 8), F32),
            jax.ShapeDtypeStruct((16, cx * 8), F32),
        ],
        scratch_shapes=[pltpu.VMEM((9, 8, cz), F32), pltpu.VMEM((6, 8, cz), F32)],
        compiler_params=pltpu.CompilerParams(
            dimension_semantics=("arbitrary",), vmem_limit_bytes=LIMIT
        ),
        name="find_edges",
    )(velocity, jnp.asarray(wa), jnp.asarray(wb))


def neighbours_kernel(gx, gz, xup, xdn, zup, zdn, xl, xr, zl, zr, send_sem, recv_sem):
    mx, mz = lax.axis_index("gx"), lax.axis_index("gz")
    xnext = (lax.rem(mx + 1, gx), mz)
    xlast = (lax.rem(mx + gx - 1, gx), mz)
    znext = (mx, lax.rem(mz + 1, gz))
    zlast = (mx, lax.rem(mz + gz - 1, gz))
    barrier = pltpu.get_barrier_semaphore()
    for peer in (xnext, xlast, znext, zlast):
        pl.semaphore_signal(barrier, inc=1, device_id=peer, device_id_type=MESH)
    pl.semaphore_wait(barrier, 4)
    moves = ((zup, zl, znext), (zdn, zr, zlast), (xup, xl, xnext), (xdn, xr, xlast))
    copies = []
    for k, (src, dst, peer) in enumerate(moves):
        copy = pltpu.make_async_remote_copy(
            src_ref=src,
            dst_ref=dst,
            send_sem=send_sem.at[k],
            recv_sem=recv_sem.at[k],
            device_id=peer,
            device_id_type=MESH,
        )
        copy.start()
        copies.append(copy)
    for copy in copies:
        copy.wait()


def swap_edges(xup, xdn, zup, zdn):
    gx, gz = lax.axis_size("gx"), lax.axis_size("gz")
    shapes = [jax.ShapeDtypeStruct(a.shape, F32) for a in (xup, xdn, zup, zdn)]
    return pl.pallas_call(
        functools.partial(neighbours_kernel, gx, gz),
        in_specs=[pl.BlockSpec(memory_space=pl.ANY)] * 4,
        out_specs=[pl.BlockSpec(memory_space=pl.ANY)] * 4,
        out_shape=shapes,
        scratch_shapes=[pltpu.SemaphoreType.DMA((4,)), pltpu.SemaphoreType.DMA((4,))],
        compiler_params=pltpu.CompilerParams(collective_id=0, has_side_effects=True),
        name="swap_edges",
    )(xup, xdn, zup, zdn)


def main_kernel(
    steps, rp_ref, v_ref, ck_ref, xl_ref, xr_ref, zl_ref, zr_ref, kh_ref, kl_ref, cm_ref, sm_ref,
    gx_ref, gz_ref, cv_ref, xs_ref, zs_ref, held, fore,
):
    t = pl.program_id(0)
    cz = v_ref.shape[3]
    rows = TX * 8

    @pl.when(t == 0)
    def _():
        fore[...] = xl_ref[...]
        xs_ref[...] = jnp.zeros_like(xs_ref)

    parts = jnp.concatenate([zl_ref[...], zr_ref[...]], 0)
    high = parts.astype(BF16).astype(F32)
    low = parts - high
    message = jnp.concatenate([high, low, high, jnp.zeros_like(high)], 0).T.astype(BF16)
    planes = [v_ref[c].reshape(rows, cz) for c in range(3)]
    for f in range(6):
        value = planes[f] if f < 3 else planes[2] * planes[f - 3]
        hi, lo = split(value)
        slope = mm(hi, kh_ref[...]) + mm(hi, kl_ref[...]) + mm(lo, kh_ref[...])
        slope = slope + mm(message, cm_ref[f])
        target = gz_ref if f < 3 else cv_ref
        target[f % 3] = slope.reshape(TX, 8, cz)

    tail = rp_ref[t]
    last = t == steps - 1
    after = [jnp.where(last, xr_ref[6 + c], ck_ref[0, 6 + c]) for c in range(3)]
    start = [ck_ref[0, c] + tail * xr_ref[c] for c in range(6)]

    def backward(k, state):
        states, nexts = list(state[:6]), list(state[6:])
        for j in range(STEP):
            i = TX - 1 - (k * STEP + j)
            for f in range(6):
                held[f, i] = -C * states[f] - KAPPA * nexts[f]
            nexts = fields([v_ref[c, i] for c in range(3)], 0)
            states = [ROOT * (f + b) for f, b in zip(nexts, states)]
        return tuple(states) + tuple(nexts)

    lax.fori_loop(0, TX // STEP, backward, tuple(start) + tuple(fields(after, 0)))

    def forward(k, state):
        states, befores = list(state[:6]), list(state[6:12])
        sums, moments = state[12], state[13]
        for j in range(STEP):
            i = k * STEP + j
            for f in range(6):
                slope = C * states[f] + (KAPPA * befores[f] + held[f, i])
                if f < 3:
                    gx_ref[f, i] = slope
                else:
                    cv_ref[f - 3, i] = cv_ref[f - 3, i] + slope
            befores = fields([v_ref[c, i] for c in range(3)], 0)
            states = [ROOT * (f + b) for f, b in zip(befores, states)]
            w_slope = gz_ref[2, i]
            sums = sums + w_slope
            moments = moments + (t * TX + i).astype(F32) * w_slope
        return tuple(states) + tuple(befores) + (sums, moments)

    begin = tuple(fore[c] for c in range(6)) + tuple(fields([fore[6 + c] for c in range(3)], 0))
    ended = lax.fori_loop(0, TX // STEP, forward, begin + (xs_ref[0], xs_ref[1]))
    for c in range(6):
        fore[c] = ended[c]
    for c in range(3):
        fore[6 + c] = ended[6 + c]
    xs_ref[0] = ended[12]
    xs_ref[1] = ended[13]

    hi, lo = split(gx_ref[0].reshape(rows, cz))
    sums = (mm(hi, sm_ref[...]) + mm(lo, sm_ref[...])).T
    chunks = [sums[q : q + 1, 128 * k : 128 * k + 128] for q in range(2) for k in range(rows // 128)]
    zs_ref[0] = jnp.concatenate(chunks, 0)


def differentiate(velocity, ck, xl, xr, zl, zr):
    _, cx, ny, cz = velocity.shape
    steps = cx // TX
    rows = TX * 8
    kh, kl = derivative_matrices(cz)
    cm = correction_matrices(cz)
    sm = np.zeros((cz, 128), ml_dtypes.bfloat16)
    sm[:, 0] = 1.0
    sm[:, 1] = np.arange(cz)
    powers = signed_power(TX * (steps - 1 - np.arange(steps))).astype(np.float32)
    whole = lambda shape: pl.BlockSpec(shape, lambda t: (0,) * len(shape))
    tile = pl.BlockSpec((3, TX, 8, cz), lambda t: (0, t, 0, 0))
    line = pl.BlockSpec((16, rows), lambda t: (0, t))
    full = jax.ShapeDtypeStruct(velocity.shape, F32)
    return pl.pallas_call(
        functools.partial(main_kernel, steps),
        grid=(steps,),
        in_specs=[
            pl.BlockSpec(memory_space=pltpu.SMEM),
            tile,
            pl.BlockSpec((1, 9, 8, cz), lambda t: (t, 0, 0, 0)),
            whole((9, 8, cz)),
            whole((9, 8, cz)),
            line,
            line,
            whole((cz, cz)),
            whole((cz, cz)),
            whole((6, 128, cz)),
            whole((cz, 128)),
        ],
        out_specs=[
            tile,
            tile,
            tile,
            whole((2, 8, cz)),
            pl.BlockSpec((1, rows // 64, 128), lambda t: (t, 0, 0)),
        ],
        out_shape=[
            full,
            full,
            full,
            jax.ShapeDtypeStruct((2, 8, cz), F32),
            jax.ShapeDtypeStruct((steps, rows // 64, 128), F32),
        ],
        scratch_shapes=[pltpu.VMEM((6, TX, 8, cz), F32), pltpu.VMEM((9, 8, cz), F32)],
        compiler_params=pltpu.CompilerParams(
            dimension_semantics=("arbitrary",), vmem_limit_bytes=LIMIT
        ),
        name="differentiate",
    )(
        jnp.asarray(powers), velocity, ck, xl, xr, zl, zr,
        jnp.asarray(kh), jnp.asarray(kl), jnp.asarray(cm), jnp.asarray(sm),
    )


def gather_kernel(gx, gz, xs, zs, xg, zg, own_sem, send_x, recv_x, send_z, recv_z):
    mx, mz = lax.axis_index("gx"), lax.axis_index("gz")
    xpeers = [(lax.rem(mx + k, gx), mz) for k in range(1, gx)]
    zpeers = [(mx, lax.rem(mz + k, gz)) for k in range(1, gz)]
    barrier = pltpu.get_barrier_semaphore()
    for peer in xpeers + zpeers:
        pl.semaphore_signal(barrier, inc=1, device_id=peer, device_id_type=MESH)
    own = [
        pltpu.make_async_copy(xs, xg.at[mx], own_sem.at[0]),
        pltpu.make_async_copy(zs, zg.at[mz], own_sem.at[1]),
    ]
    for copy in own:
        copy.start()
    pl.semaphore_wait(barrier, gx + gz - 2)
    copies = []
    for src, dst, mine, peers, sends, recvs in (
        (zs, zg, mz, zpeers, send_z, recv_z),
        (xs, xg, mx, xpeers, send_x, recv_x),
    ):
        for k, peer in enumerate(peers):
            copy = pltpu.make_async_remote_copy(
                src_ref=src,
                dst_ref=dst.at[mine],
                send_sem=sends.at[k],
                recv_sem=recvs.at[k],
                device_id=peer,
                device_id_type=MESH,
            )
            copy.start()
            copies.append(copy)
    for copy in own + copies:
        copy.wait()


def gather_sums(xs, zs):
    gx, gz = lax.axis_size("gx"), lax.axis_size("gz")
    dma = pltpu.SemaphoreType.DMA
    return pl.pallas_call(
        functools.partial(gather_kernel, gx, gz),
        in_specs=[pl.BlockSpec(memory_space=pl.ANY)] * 2,
        out_specs=[pl.BlockSpec(memory_space=pl.ANY)] * 2,
        out_shape=[
            jax.ShapeDtypeStruct((gx,) + xs.shape, F32),
            jax.ShapeDtypeStruct((gz,) + zs.shape, F32),
        ],
        scratch_shapes=[
            dma((2,)), dma((gx - 1,)), dma((gx - 1,)), dma((gz - 1,)), dma((gz - 1,))
        ],
        compiler_params=pltpu.CompilerParams(collective_id=1, has_side_effects=True),
        name="gather_sums",
    )(xs, zs)


def rebuild_kernel(
    nx, nz, wx_ref, wz_ref, xg_ref, zg_ref, tm_ref, pm_ref, gzw_ref, gxu_ref, out_ref, run, mean
):
    t = pl.program_id(0)
    cz = gzw_ref.shape[3]
    rows = TX * 8
    scale_x, scale_z = -1.0 / math.sqrt(nx), -1.0 / math.sqrt(nz)

    @pl.when(t == 0)
    def _():
        base = jnp.zeros((8, cz), F32)
        average = jnp.zeros((8, cz), F32)
        for d in range(xg_ref.shape[0]):
            base = base + wx_ref[d] * xg_ref[d, 0] + xg_ref[d, 1] * (1.0 / nx)
            average = average + xg_ref[d, 0] * (1.0 / nx)
        run[...] = base
        mean[...] = average

    average = mean[...]

    def forward(k, total):
        for j in range(STEP):
            i = k * STEP + j
            value = gzw_ref[0, i]
            out_ref[0, i] = scale_x * (total + 0.5 * value)
            total = total + (value - average)
        return total

    run[...] = lax.fori_loop(0, TX // STEP, forward, run[...])

    chunks = rows // 128
    base = jnp.zeros((chunks, 128), F32)
    slope = jnp.zeros((chunks, 128), F32)
    for d in range(zg_ref.shape[0]):
        block = zg_ref[d, 0]
        base = base + wz_ref[d] * block[0:chunks] + block[chunks:] * (1.0 / nz)
        slope = slope + block[0:chunks] * (1.0 / nz)
    base = jnp.concatenate([base[k : k + 1] for k in range(chunks)], 1)
    slope = jnp.concatenate([slope[k : k + 1] for k in range(chunks)], 1)
    base_high = base.astype(BF16).astype(F32)
    slope_high = slope.astype(BF16).astype(F32)
    stacked = jnp.concatenate(
        [base_high, base - base_high, slope_high, slope - slope_high, jnp.zeros((124, rows), F32)], 0
    )
    message = stacked.T.astype(BF16)
    hi, lo = split(gxu_ref[0].reshape(rows, cz))
    result = mm(hi, tm_ref[...]) + mm(lo, tm_ref[...]) + mm(message, pm_ref[...])
    out_ref[1] = (scale_z * result).reshape(TX, 8, cz)


def start_weights(axis, cells):
    peers, mine = lax.axis_size(axis), lax.axis_index(axis)
    total = peers * cells
    at = jnp.arange(peers)
    starts = (at * cells - mine * cells).astype(F32)
    return (at < mine).astype(F32) + (starts - 0.5 * (total - 1) - 0.5) * (1.0 / total)


def rebuild(grad_x, grad_z, xg, zg):
    _, cx, ny, cz = grad_x.shape
    gx, gz = xg.shape[0], zg.shape[0]
    steps = cx // TX
    rows = TX * 8
    at = np.arange(cz)
    tm = (at[:, None] < at[None, :]) + 0.5 * (at[:, None] == at[None, :])
    pm = np.zeros((128, cz))
    pm[0:2] = 1.0
    pm[2:4] = -at
    whole = lambda shape: pl.BlockSpec(shape, lambda t: (0,) * len(shape))
    return pl.pallas_call(
        functools.partial(rebuild_kernel, cx * gx, cz * gz),
        grid=(steps,),
        in_specs=[
            pl.BlockSpec(memory_space=pltpu.SMEM),
            pl.BlockSpec(memory_space=pltpu.SMEM),
            whole((gx, 2, 8, cz)),
            pl.BlockSpec((gz, 1, rows // 64, 128), lambda t: (0, t, 0, 0)),
            whole((cz, cz)),
            whole((128, cz)),
            pl.BlockSpec((1, TX, 8, cz), lambda t: (2, t, 0, 0)),
            pl.BlockSpec((1, TX, 8, cz), lambda t: (0, t, 0, 0)),
        ],
        out_specs=pl.BlockSpec((2, TX, 8, cz), lambda t: (0, t, 0, 0)),
        out_shape=jax.ShapeDtypeStruct((2, cx, 8, cz), F32),
        scratch_shapes=[pltpu.VMEM((8, cz), F32), pltpu.VMEM((8, cz), F32)],
        compiler_params=pltpu.CompilerParams(
            dimension_semantics=("arbitrary",), vmem_limit_bytes=LIMIT
        ),
        name="rebuild",
    )(
        start_weights("gx", cx), start_weights("gz", cz), xg, zg,
        jnp.asarray(tm.astype(ml_dtypes.bfloat16)), jnp.asarray(pm.astype(ml_dtypes.bfloat16)),
        grad_z, grad_x,
    )


def body(velocity):
    ck, xup, xdn, zup, zdn = find_edges(velocity)
    xl, xr, zl, zr = swap_edges(xup, xdn, zup, zdn)
    grad_x, grad_z, convect, xs, zs = differentiate(velocity, ck, xl, xr, zl, zr)
    xg, zg = gather_sums(xs, zs)
    rebuilt = rebuild(grad_x, grad_z, xg, zg)
    return grad_x, grad_z, convect, rebuilt


def solution(mesh):
    placed = P(None, "gx", None, "gz")
    return jax.shard_map(
        body, mesh=mesh, in_specs=(placed,), out_specs=(placed,) * 4, check_vma=False
    )
```

time: 1910 us -> 101 us (0.05)
  local copies, waits for them, and re-layouts: 558 us -> 11.3 us
  waiting for transfers between devices: 543 us -> 0 us
  blocking collectives: 415 us -> 0 us
  other arithmetic: 291 us -> 0.02 us
  Pallas kernels: 0 us -> 87.9 us
  matrix products: 75.8 us -> 0 us
    all_to_all x2 -> x0, waiting for transfers between devices: 538 us -> none  [the longest x1 538 us: body(): lax.all_to_all(fields_z, 'gz', split_axis=1, concat_axis=3, tiled=True)]
    psum x2 -> x0, blocking collectives: 379 us -> none  [the longest x1 368 us: body(): line_sum_z, centred_z = lax.psum((sum_z, moment_z), 'gz')]
    slice x17 -> x0, local copies, waits for them, and re-layouts: 198 us -> none  [the longest x3 53.2 us: couple(): lax.slice_in_dim(last_cells, 0, count - 1, axis=axis_at)]
    unnamed x32 -> x42, local copies, waits for them, and re-layouts: 201 us -> 11.3 us
    pallas_call x0 -> x5, Pallas kernels: none -> 87.9 us  [the longest x1 36.3 us: differentiate(): pl.pallas_call(functools.partial(main_kernel, steps), grid=(steps,), in_s...]
    all_to_all x4 -> x0, local copies, waits for them, and re-layouts: 85.8 us -> none  [the longest x2 51.5 us: body(): lax.all_to_all(fields_z, 'gz', split_axis=1, concat_axis=3, tiled=True)]
    dot_general x18 -> x0, matrix products: 75.8 us -> none  [the longest x2 37.6 us: apply_matrix(): lax.dot_general(batched, flat, (((2,), (1,)), ((0,), (0,))), precision=la...]
    all_to_all x1 -> x0, other arithmetic: 71.2 us -> none  [body(): lax.all_to_all(solved_lines_z, 'gz', split_axis=3, concat_axis=1, tiled=T...]
  transfers between devices with their start and end apart: 6 -> 0, of which waited for: 4 -> 0; matrix products, arithmetic and copies ran while one was open for 11% -> 0% of each run, Pallas kernels for 0% -> 0%
where the time goes in v1:
time: 101 us; the launch traced here: 100 us
  Pallas kernels  87.9 us (87%)
  local copies, waits for them, and re-layouts  11.3 us (11%)
    pallas_call x1, Pallas kernels, differentiate(): pl.pallas_call(functools.partial(main_kernel, steps), grid=(steps,), in_s...  36.3 us
    pallas_call x1, Pallas kernels, swap_edges(): pl.pallas_call(functools.partial(neighbours_kernel, gx, gz), in_specs=[pl...  17.1 us
    pallas_call x1, Pallas kernels, find_edges(): pl.pallas_call(functools.partial(edges_kernel, steps), grid=(steps,), in_...  14.3 us
    unnamed x42, local copies, waits for them, and re-layouts  11.3 us
    pallas_call x1, Pallas kernels, rebuild(): pl.pallas_call(functools.partial(rebuild_kernel, cx * gx, cz * gz), grid=...  10.5 us
    pallas_call x1, Pallas kernels, gather_sums(): pl.pallas_call(functools.partial(gather_kernel, gx, gz), in_specs=[pl.Blo...  9.74 us

profile of v1, /device:TPU:0, one launch (start us, length us, event | category | flops | bytes accessed | tf_op | source)
XLA Modules:
  0.0 100.1 jit_solution(2521095850760181440)
XLA Ops:
  0.6 0.0 copy-start.20
  0.7 0.0 copy-start
  0.7 1.0 copy-done
  1.7 0.0 copy-start.1
  1.7 1.0 copy-done.1
  2.7 0.0 copy-start.2
  2.7 0.0 copy-start.9
  2.7 0.0 copy-start.10
  2.7 0.0 copy-start.16
  2.7 0.0 copy-start.8
  2.7 0.0 copy-start.15
  2.7 14.3 %find_edges.1 = (f32[8,9,8,256]{3,2,1,0:T(8,128)}, f32[9,8,256]{2,1,0:T(8,128)S(1)}, f32[9,8,256]{2,1,0:T(8,128)S(1)}, f32[16,4096]{1,0:T(8,128)S(1)}, f32[16,4096]{1,0:T(8,128)S(1)}) custom-call(f32[3,512,8,256]{3,2,1,0:T(8,128)} %v_ref.3, bf16[6,256,128]{2,1,0:T(8,128)(2,1)S(1)} %copy-done.1, bf16[6,256,128]{2,1,0:T(8,128)(2,1)S(1)} %copy-done), custom_call_target="tpu_custom_call" | custom-call | tf_op jit(solution)/shard_map/find_edges/pallas_call | solution.py:159
  17.0 0.0 copy-start.6
  17.0 0.7 copy-done.6
  17.7 0.0 copy-start.7
  17.7 0.7 copy-done.7
  18.4 0.0 copy-start.13
  18.4 0.6 copy-done.13
  19.0 0.0 copy-start.14
  19.0 0.6 copy-done.14
  19.6 17.1 %swap_edges.1 = (f32[9,8,256]{2,1,0:T(8,128)}, f32[9,8,256]{2,1,0:T(8,128)}, f32[16,4096]{1,0:T(8,128)}, f32[16,4096]{1,0:T(8,128)}) custom-call(f32[9,8,256]{2,1,0:T(8,128)} %copy-done.13, f32[9,8,256]{2,1,0:T(8,128)} %copy-done.14, f32[16,4096]{1,0:T(8,128)} %copy-done.6, f32[16,4096]{1,0:T(8,128)} %copy-done.7), custom_call_target="tpu_custom_call" | custom-call | tf_op jit(solution)/shard_map/swap_edges/pallas_call | solution.py:219
  36.7 0.0 copy-done.20
  36.7 0.0 copy-done.2
  36.7 0.0 copy-done.9
  36.7 0.0 copy-done.10
  36.7 0.0 copy-done.16
  36.8 0.0 copy-start.3
  36.8 0.9 copy-done.3
  37.7 0.0 copy-start.4
  37.7 0.9 copy-done.4
  38.7 0.0 copy-start.11
  38.7 0.9 copy-done.11
  39.5 0.0 copy-start.12
  39.5 0.9 copy-done.12
  40.4 36.3 %differentiate.1 = (f32[3,512,8,256]{3,2,1,0:T(8,128)}, f32[3,512,8,256]{3,2,1,0:T(8,128)}, f32[3,512,8,256]{3,2,1,0:T(8,128)}, f32[2,8,256]{2,1,0:T(8,128)S(1)}, f32[8,8,128]{2,1,0:T(8,128)S(1)}) custom-call(f32[8]{0:T(128)S(1)} %copy-done.20, f32[3,512,8,256]{3,2,1,0:T(8,128)} %v_ref.3, f32[8,9,8,256]{3,2,1,0:T(8,128)} %get-tuple-element.20.ck_ref, ...), custom_call_target="tpu_custom_call" | custom-call | tf_op jit(solution)/shard_map/differentiate/pallas_call | solution.py:320
  76.8 0.0 copy-start.18
  76.8 0.6 copy-done.18
  77.4 0.0 copy-start.19
  77.4 0.6 copy-done.19
  78.0 9.7 %gather_sums.1 = (f32[4,2,8,256]{3,2,1,0:T(8,128)}, f32[8,8,8,128]{3,2,1,0:T(8,128)}) custom-call(f32[2,8,256]{2,1,0:T(8,128)} %copy-done.19, f32[8,8,128]{2,1,0:T(8,128)} %copy-done.18), custom_call_target="tpu_custom_call" | custom-call | tf_op jit(solution)/shard_map/gather_sums/pallas_call | solution.py:398
  87.7 0.0 copy-done.8
  87.7 0.0 copy-done.15
  87.7 0.0 copy-start.5
  87.7 0.9 copy-done.5
  88.7 0.0 copy-start.17
  88.7 0.8 copy-done.17
  89.5 10.5 %rebuild.1 = f32[2,512,8,256]{3,2,1,0:T(8,128)} custom-call(f32[4]{0:T(128)S(1)} %fusion.wx_ref, f32[8]{0:T(128)S(1)} %fusion.1.wz_ref, f32[4,2,8,256]{3,2,1,0:T(8,128)S(1)} %copy-done.17, f32[8,8,8,128]{3,2,1,0:T(8,128)S(1)} %copy-done.5, bf16[256,256]{1,0:T(8,128)(2,1)S(1)} %copy-done.8, bf16[128,256]{1,0:T(8,128)(2,1)S(1)} %copy-done.15, ...), custom_call_target="tpu_custom_call" | custom-call | tf_op jit(solution)/shard_map/rebuild/pallas_call | solution.py:483
  (2 shorter events, 0.0 us)
Async XLA Ops:
  0.6 36.1 %copy-start.20 = (f32[8]{0:T(128)S(1)}, f32[8]{0:T(128)}, u32[]{:S(2)}) copy-start(f32[8]{0:T(128)} %constant.48.clone.rp_ref) | copy-start | bytes 100
  0.7 1.0 copy-start
  1.7 1.0 copy-start.1
  2.7 34.0 %copy-start.2 = (bf16[6,128,256]{2,1,0:T(8,128)(2,1)S(1)}, bf16[6,128,256]{2,1,0:T(8,128)(2,1)}, u32[]{:S(2)}) copy-start(bf16[6,128,256]{2,1,0:T(8,128)(2,1)} %constant.51.clone.cm_ref) | copy-start | bytes 1179652
  2.7 34.1 %copy-start.9 = (bf16[256,256]{1,0:T(8,128)(2,1)S(1)}, bf16[256,256]{1,0:T(8,128)(2,1)}, u32[]{:S(2)}) copy-start(bf16[256,256]{1,0:T(8,128)(2,1)} %constant.50.clone.kl_ref) | copy-start | bytes 393220
  2.7 34.1 %copy-start.10 = (bf16[256,256]{1,0:T(8,128)(2,1)S(1)}, bf16[256,256]{1,0:T(8,128)(2,1)}, u32[]{:S(2)}) copy-start(bf16[256,256]{1,0:T(8,128)(2,1)} %constant.49.clone.kh_ref) | copy-start | bytes 393220
  2.7 34.1 %copy-start.16 = (bf16[256,128]{1,0:T(8,128)(2,1)S(1)}, bf16[256,128]{1,0:T(8,128)(2,1)}, u32[]{:S(2)}) copy-start(bf16[256,128]{1,0:T(8,128)(2,1)} %constant.52.clone.sm_ref) | copy-start | bytes 196612
  2.7 85.0 %copy-start.8 = (bf16[256,256]{1,0:T(8,128)(2,1)S(1)}, bf16[256,256]{1,0:T(8,128)(2,1)}, u32[]{:S(2)}) copy-start(bf16[256,256]{1,0:T(8,128)(2,1)} %constant.53.clone.tm_ref) | copy-start | bytes 393220
  2.7 85.0 %copy-start.15 = (bf16[128,256]{1,0:T(8,128)(2,1)S(1)}, bf16[128,256]{1,0:T(8,128)(2,1)}, u32[]{:S(2)}) copy-start(bf16[128,256]{1,0:T(8,128)(2,1)} %constant.54.clone.pm_ref) | copy-start | bytes 196612
  17.0 0.7 copy-start.6
  17.7 0.7 copy-start.7
  18.4 0.6 copy-start.13
  19.0 0.6 copy-start.14
  36.8 1.0 copy-start.3
  37.7 0.9 copy-start.4
  38.7 0.9 copy-start.11
  39.5 0.9 copy-start.12
  76.8 0.6 copy-start.18
  77.4 0.6 copy-start.19
  87.7 1.0 copy-start.5
  88.7 0.8 copy-start.17

commit v2 on v1

--- a/solution.py
+++ b/solution.py
@@ -14,7 +14,8 @@
 C = 25.0 / 12.0
 KAPPA = -1.0 / 12.0
 TX = 64
-STEP = 4
+CHUNK = 16
+STEP = 8
 F32 = jnp.float32
 BF16 = jnp.bfloat16
 LIMIT = 52 * 1024 * 1024
@@ -55,19 +56,16 @@
 
 def edge_weights(cz):
     at = np.arange(cz)
-    out = np.zeros((6, cz, 128))
-    low_out = np.zeros((6, cz, 128))
-    for f in range(6):
-        base = np.zeros((cz, 32))
-        base[:, f] = signed_power(cz - at)
-        base[cz - 1, 6 + f] = 1.0
-        base[:, 16 + f] = signed_power(at + 1)
-        base[0, 22 + f] = 1.0
-        high, low = halves(base)
-        out[f, :, 0:32] = high.astype(np.float64)
-        out[f, :, 32:64] = low.astype(np.float64)
-        low_out[f, :, 0:32] = high.astype(np.float64)
-    return out.astype(ml_dtypes.bfloat16), low_out.astype(ml_dtypes.bfloat16)
+    base = np.zeros((cz, 32))
+    base[:, 0] = signed_power(cz - at)
+    base[cz - 1, 6] = 1.0
+    base[:, 16] = signed_power(at + 1)
+    base[0, 22] = 1.0
+    high, low = halves(base)
+    out = np.zeros((cz, 128), np.float32)
+    out[:, 0:32] = high.astype(np.float32)
+    out[:, 32:64] = low.astype(np.float32)
+    return out
 
 
 def correction_matrices(cz):
@@ -90,28 +88,52 @@
     return list(planes) + [planes[pivot] * p for p in planes]
 
 
-def edges_kernel(steps, v_ref, wa_ref, wb_ref, ck_ref, xup_ref, xdn_ref, zup_ref, zdn_ref, back, fore):
+def chunk_operands(v_ref, begin):
+    cz = v_ref.shape[3]
+    planes = [v_ref[c, pl.ds(begin, CHUNK)].reshape(CHUNK * 8, cz) for c in range(3)]
+    return [split(value) for value in fields(planes, 2)]
+
+
+def edges_kernel(
+    steps, v_ref, w_ref, ck_ref, xup_ref, xdn_ref, zup_ref, zdn_ref, wup_ref, wdn_ref, back, fore, mat
+):
     s = pl.program_id(0)
     cz = v_ref.shape[3]
-    rows = TX * 8
 
     @pl.when(s == 0)
     def _():
         back[...] = jnp.zeros_like(back)
         fore[...] = jnp.zeros_like(fore)
         xup_ref[6:9] = v_ref[:, TX - 1]
+        base = w_ref[...]
+        lane = lax.broadcasted_iota(jnp.int32, base.shape, 1)
+        for f in range(6):
+            turned = base if f == 0 else pltpu.roll(base, f, 1)
+            mat[2 * f * cz : (2 * f + 1) * cz] = turned.astype(BF16)
+            mat[(2 * f + 1) * cz : (2 * f + 2) * cz] = jnp.where(lane < 32, turned, 0.0).astype(BF16)
 
     ck_ref[0] = back[...]
 
     def sweep(k, state):
+        begin = pl.multiple_of(TX - (k + 1) * CHUNK, CHUNK)
+        operands = chunk_operands(v_ref, begin)
+        joined = jnp.concatenate([part for pair in operands for part in pair], 1)
+        turned = mm(joined, mat[...]).T
+        message = turned[0:32] + turned[32:64]
+        at = pl.ds(pl.multiple_of(begin * 8, CHUNK * 8), CHUNK * 8)
+        zup_ref[:, at] = message[0:8]
+        zdn_ref[:, at] = message[16:24]
+        spot = pl.ds(TX // CHUNK - 1 - k, 1)
+        wup_ref[0, spot] = message[8:9]
+        wdn_ref[0, spot] = message[24:25]
         states = list(state)
-        for j in range(STEP):
-            i = TX - 1 - (k * STEP + j)
+        for j in range(CHUNK):
+            i = begin + (CHUNK - 1 - j)
             now = fields([v_ref[c, i] for c in range(3)], 0)
             states = [ROOT * (f + b) for f, b in zip(now, states)]
         return tuple(states)
 
-    final = lax.fori_loop(0, TX // STEP, sweep, tuple(back[c] for c in range(6)))
+    final = lax.fori_loop(0, TX // CHUNK, sweep, tuple(back[c] for c in range(6)))
     for c in range(6):
         back[c] = final[c]
     back[6:9] = v_ref[:, 0]
@@ -132,17 +154,6 @@
         for c in range(6):
             fore[c] = fore[c] + scale * ended[c]
 
-    planes = [v_ref[c].reshape(rows, cz) for c in range(3)]
-    total = jnp.zeros((rows, 128), F32)
-    for f in range(6):
-        value = planes[f] if f < 3 else planes[2] * planes[f - 3]
-        high, low = split(value)
-        total = total + mm(high, wa_ref[f]) + mm(low, wb_ref[f])
-    turned = total.T
-    message = turned[0:32] + turned[32:64]
-    zup_ref[...] = message[0:16]
-    zdn_ref[...] = message[16:32]
-
     @pl.when(s == steps - 1)
     def _():
         xup_ref[0:6] = fore[...]
@@ -153,40 +164,47 @@
     _, cx, ny, cz = velocity.shape
     steps = cx // TX
     rows = TX * 8
-    wa, wb = edge_weights(cz)
     whole = lambda shape: pl.BlockSpec(shape, lambda s: (0,) * len(shape))
-    turned = lambda s: (0, steps - 1 - s)
+    line = pl.BlockSpec((8, rows), lambda s: (0, steps - 1 - s))
+    short = pl.BlockSpec((1, rows // 128, 128), lambda s: (steps - 1 - s, 0, 0))
     return pl.pallas_call(
         functools.partial(edges_kernel, steps),
         grid=(steps,),
         in_specs=[
             pl.BlockSpec((3, TX, 8, cz), lambda s: (0, steps - 1 - s, 0, 0)),
-            whole((6, cz, 128)),
-            whole((6, cz, 128)),
+            whole((cz, 128)),
         ],
         out_specs=[
             pl.BlockSpec((1, 9, 8, cz), lambda s: (steps - 1 - s, 0, 0, 0)),
             whole((9, 8, cz)),
             whole((9, 8, cz)),
-            pl.BlockSpec((16, rows), turned),
-            pl.BlockSpec((16, rows), turned),
+            line,
+            line,
+            short,
+            short,
         ],
         out_shape=[
             jax.ShapeDtypeStruct((steps, 9, 8, cz), F32),
             jax.ShapeDtypeStruct((9, 8, cz), F32),
             jax.ShapeDtypeStruct((9, 8, cz), F32),
-            jax.ShapeDtypeStruct((16, cx * 8), F32),
-            jax.ShapeDtypeStruct((16, cx * 8), F32),
-        ],
-        scratch_shapes=[pltpu.VMEM((9, 8, cz), F32), pltpu.VMEM((6, 8, cz), F32)],
+            jax.ShapeDtypeStruct((8, cx * 8), F32),
+            jax.ShapeDtypeStruct((8, cx * 8), F32),
+            jax.ShapeDtypeStruct((steps, rows // 128, 128), F32),
+            jax.ShapeDtypeStruct((steps, rows // 128, 128), F32),
+        ],
+        scratch_shapes=[
+            pltpu.VMEM((9, 8, cz), F32),
+            pltpu.VMEM((6, 8, cz), F32),
+            pltpu.VMEM((12 * cz, 128), BF16),
+        ],
         compiler_params=pltpu.CompilerParams(
             dimension_semantics=("arbitrary",), vmem_limit_bytes=LIMIT
         ),
         name="find_edges",
-    )(velocity, jnp.asarray(wa), jnp.asarray(wb))
-
-
-def neighbours_kernel(gx, gz, xup, xdn, zup, zdn, xl, xr, zl, zr, send_sem, recv_sem):
+    )(velocity, jnp.asarray(edge_weights(cz)))
+
+
+def neighbours_kernel(gx, gz, xup, xdn, zup, zdn, wup, wdn, xl, xr, zl, zr, wl, wr, send_sem, recv_sem):
     mx, mz = lax.axis_index("gx"), lax.axis_index("gz")
     xnext = (lax.rem(mx + 1, gx), mz)
     xlast = (lax.rem(mx + gx - 1, gx), mz)
@@ -196,7 +214,14 @@
     for peer in (xnext, xlast, znext, zlast):
         pl.semaphore_signal(barrier, inc=1, device_id=peer, device_id_type=MESH)
     pl.semaphore_wait(barrier, 4)
-    moves = ((zup, zl, znext), (zdn, zr, zlast), (xup, xl, xnext), (xdn, xr, xlast))
+    moves = (
+        (zup, zl, znext),
+        (zdn, zr, zlast),
+        (wup, wl, znext),
+        (wdn, wr, zlast),
+        (xup, xl, xnext),
+        (xdn, xr, xlast),
+    )
     copies = []
     for k, (src, dst, peer) in enumerate(moves):
         copy = pltpu.make_async_remote_copy(
@@ -213,87 +238,105 @@
         copy.wait()
 
 
-def swap_edges(xup, xdn, zup, zdn):
+def swap_edges(*arrays):
     gx, gz = lax.axis_size("gx"), lax.axis_size("gz")
-    shapes = [jax.ShapeDtypeStruct(a.shape, F32) for a in (xup, xdn, zup, zdn)]
+    count = len(arrays)
     return pl.pallas_call(
         functools.partial(neighbours_kernel, gx, gz),
-        in_specs=[pl.BlockSpec(memory_space=pl.ANY)] * 4,
-        out_specs=[pl.BlockSpec(memory_space=pl.ANY)] * 4,
-        out_shape=shapes,
-        scratch_shapes=[pltpu.SemaphoreType.DMA((4,)), pltpu.SemaphoreType.DMA((4,))],
-        compiler_params=pltpu.CompilerParams(collective_id=0, has_side_effects=True),
+        in_specs=[pl.BlockSpec(memory_space=pltpu.VMEM)] * count,
+        out_specs=[pl.BlockSpec(memory_space=pltpu.VMEM)] * count,
+        out_shape=[jax.ShapeDtypeStruct(a.shape, F32) for a in arrays],
+        scratch_shapes=[pltpu.SemaphoreType.DMA((count,)), pltpu.SemaphoreType.DMA((count,))],
+        compiler_params=pltpu.CompilerParams(
+            collective_id=0, has_side_effects=True, vmem_limit_bytes=8 * 1024 * 1024
+        ),
         name="swap_edges",
-    )(xup, xdn, zup, zdn)
+    )(*arrays)
 
 
 def main_kernel(
-    steps, rp_ref, v_ref, ck_ref, xl_ref, xr_ref, zl_ref, zr_ref, kh_ref, kl_ref, cm_ref, sm_ref,
-    gx_ref, gz_ref, cv_ref, xs_ref, zs_ref, held, fore,
+    steps, rp_ref, v_ref, ck_ref, xl_ref, xr_ref, zl_ref, zr_ref, wl_ref, wr_ref, km_ref, cm_ref, sm_ref,
+    gx_ref, gz_ref, cv_ref, xs_ref, zs_ref, held, fore, msg,
 ):
     t = pl.program_id(0)
     cz = v_ref.shape[3]
     rows = TX * 8
+    gain = C * ROOT / KAPPA
 
     @pl.when(t == 0)
     def _():
-        fore[...] = xl_ref[...]
+        for f, edge in enumerate(fields([xl_ref[6 + c] for c in range(3)], 0)):
+            fore[f] = C * xl_ref[f]
+            fore[6 + f] = KAPPA * edge + C * xl_ref[f]
         xs_ref[...] = jnp.zeros_like(xs_ref)
 
-    parts = jnp.concatenate([zl_ref[...], zr_ref[...]], 0)
+    parts = []
+    for main, short in ((zl_ref, wl_ref), (zr_ref, wr_ref)):
+        lines = main[...]
+        edge_w = jnp.concatenate([short[0, k : k + 1] for k in range(rows // 128)], 1)
+        parts += [lines, edge_w, edge_w * lines[6:7], edge_w * lines[7:8], edge_w * edge_w]
+        parts.append(jnp.zeros((4, rows), F32))
+    parts = jnp.concatenate(parts, 0)
     high = parts.astype(BF16).astype(F32)
     low = parts - high
-    message = jnp.concatenate([high, low, high, jnp.zeros_like(high)], 0).T.astype(BF16)
-    planes = [v_ref[c].reshape(rows, cz) for c in range(3)]
-    for f in range(6):
-        value = planes[f] if f < 3 else planes[2] * planes[f - 3]
-        hi, lo = split(value)
-        slope = mm(hi, kh_ref[...]) + mm(hi, kl_ref[...]) + mm(lo, kh_ref[...])
-        slope = slope + mm(message, cm_ref[f])
-        target = gz_ref if f < 3 else cv_ref
-        target[f % 3] = slope.reshape(TX, 8, cz)
+    msg[...] = jnp.concatenate([high, low, high, jnp.zeros_like(high)], 0).T.astype(BF16)
 
     tail = rp_ref[t]
     last = t == steps - 1
     after = [jnp.where(last, xr_ref[6 + c], ck_ref[0, 6 + c]) for c in range(3)]
-    start = [ck_ref[0, c] + tail * xr_ref[c] for c in range(6)]
+    start = [C * (ck_ref[0, c] + tail * xr_ref[c]) for c in range(6)]
+    shown = [KAPPA * f + b for f, b in zip(fields(after, 0), start)]
+
+    def scaled(i):
+        planes = [v_ref[c, i] for c in range(3)]
+        scaled_planes = [KAPPA * p for p in planes]
+        return scaled_planes + [scaled_planes[0] * p for p in planes]
 
     def backward(k, state):
-        states, nexts = list(state[:6]), list(state[6:])
-        for j in range(STEP):
-            i = TX - 1 - (k * STEP + j)
+        begin = pl.multiple_of(TX - (k + 1) * CHUNK, CHUNK)
+        operands = chunk_operands(v_ref, begin)
+        joined = jnp.concatenate([jnp.concatenate([hi, hi, lo], 1) for hi, lo in operands], 0)
+        slopes = mm(joined, km_ref[...])
+        fixes = mm(msg[pl.ds(pl.multiple_of(begin * 8, CHUNK * 8), CHUNK * 8)], cm_ref[...])
+        for f in range(6):
+            slope = slopes[f * CHUNK * 8 : (f + 1) * CHUNK * 8] + fixes[:, f * cz : (f + 1) * cz]
+            target = gz_ref if f < 3 else cv_ref
+            target[f % 3, pl.ds(begin, CHUNK)] = slope.reshape(CHUNK, 8, cz)
+        states, outs = list(state[:6]), list(state[6:])
+        for j in range(CHUNK):
+            i = begin + (CHUNK - 1 - j)
             for f in range(6):
-                held[f, i] = -C * states[f] - KAPPA * nexts[f]
-            nexts = fields([v_ref[c, i] for c in range(3)], 0)
-            states = [ROOT * (f + b) for f, b in zip(nexts, states)]
-        return tuple(states) + tuple(nexts)
-
-    lax.fori_loop(0, TX // STEP, backward, tuple(start) + tuple(fields(after, 0)))
+                held[f, i] = outs[f]
+            now = scaled(i)
+            states = [gain * f + ROOT * b for f, b in zip(now, states)]
+            outs = [f + b for f, b in zip(now, states)]
+        return tuple(states) + tuple(outs)
+
+    lax.fori_loop(0, TX // CHUNK, backward, tuple(start) + tuple(shown))
 
     def forward(k, state):
-        states, befores = list(state[:6]), list(state[6:12])
+        states, outs = list(state[:6]), list(state[6:12])
         sums, moments = state[12], state[13]
         for j in range(STEP):
             i = k * STEP + j
             for f in range(6):
-                slope = C * states[f] + (KAPPA * befores[f] + held[f, i])
+                slope = outs[f] - held[f, i]
                 if f < 3:
                     gx_ref[f, i] = slope
                 else:
                     cv_ref[f - 3, i] = cv_ref[f - 3, i] + slope
-            befores = fields([v_ref[c, i] for c in range(3)], 0)
-            states = [ROOT * (f + b) for f, b in zip(befores, states)]
+            now = scaled(i)
+            states = [gain * f + ROOT * b for f, b in zip(now, states)]
+            outs = [f + b for f, b in zip(now, states)]
             w_slope = gz_ref[2, i]
             sums = sums + w_slope
             moments = moments + (t * TX + i).astype(F32) * w_slope
-        return tuple(states) + tuple(befores) + (sums, moments)
-
-    begin = tuple(fore[c] for c in range(6)) + tuple(fields([fore[6 + c] for c in range(3)], 0))
+        return tuple(states) + tuple(outs) + (sums, moments)
+
+    begin = tuple(fore[c] for c in range(12))
     ended = lax.fori_loop(0, TX // STEP, forward, begin + (xs_ref[0], xs_ref[1]))
-    for c in range(6):
+    for c in range(12):
         fore[c] = ended[c]
-    for c in range(3):
-        fore[6 + c] = ended[6 + c]
     xs_ref[0] = ended[12]
     xs_ref[1] = ended[13]
 
@@ -303,19 +346,21 @@
     zs_ref[0] = jnp.concatenate(chunks, 0)
 
 
-def differentiate(velocity, ck, xl, xr, zl, zr):
+def differentiate(velocity, ck, xl, xr, zl, zr, wl, wr):
     _, cx, ny, cz = velocity.shape
     steps = cx // TX
     rows = TX * 8
     kh, kl = derivative_matrices(cz)
-    cm = correction_matrices(cz)
+    km = np.concatenate([kh, kl, kh], 0)
+    cm = np.concatenate(list(correction_matrices(cz)), 1)
     sm = np.zeros((cz, 128), ml_dtypes.bfloat16)
     sm[:, 0] = 1.0
     sm[:, 1] = np.arange(cz)
     powers = signed_power(TX * (steps - 1 - np.arange(steps))).astype(np.float32)
     whole = lambda shape: pl.BlockSpec(shape, lambda t: (0,) * len(shape))
     tile = pl.BlockSpec((3, TX, 8, cz), lambda t: (0, t, 0, 0))
-    line = pl.BlockSpec((16, rows), lambda t: (0, t))
+    line = pl.BlockSpec((8, rows), lambda t: (0, t))
+    short = pl.BlockSpec((1, rows // 128, 128), lambda t: (t, 0, 0))
     full = jax.ShapeDtypeStruct(velocity.shape, F32)
     return pl.pallas_call(
         functools.partial(main_kernel, steps),
@@ -328,9 +373,10 @@
             whole((9, 8, cz)),
             line,
             line,
-            whole((cz, cz)),
-            whole((cz, cz)),
-            whole((6, 128, cz)),
+            short,
+            short,
+            whole((3 * cz, cz)),
+            whole((128, 6 * cz)),
             whole((cz, 128)),
         ],
         out_specs=[
@@ -347,14 +393,18 @@
             jax.ShapeDtypeStruct((2, 8, cz), F32),
             jax.ShapeDtypeStruct((steps, rows // 64, 128), F32),
         ],
-        scratch_shapes=[pltpu.VMEM((6, TX, 8, cz), F32), pltpu.VMEM((9, 8, cz), F32)],
+        scratch_shapes=[
+            pltpu.VMEM((6, TX, 8, cz), F32),
+            pltpu.VMEM((12, 8, cz), F32),
+            pltpu.VMEM((rows, 128), BF16),
+        ],
         compiler_params=pltpu.CompilerParams(
             dimension_semantics=("arbitrary",), vmem_limit_bytes=LIMIT
         ),
         name="differentiate",
     )(
-        jnp.asarray(powers), velocity, ck, xl, xr, zl, zr,
-        jnp.asarray(kh), jnp.asarray(kl), jnp.asarray(cm), jnp.asarray(sm),
+        jnp.asarray(powers), velocity, ck, xl, xr, zl, zr, wl, wr,
+        jnp.asarray(km), jnp.asarray(cm), jnp.asarray(sm),
     )
 
 
@@ -397,8 +447,8 @@
     dma = pltpu.SemaphoreType.DMA
     return pl.pallas_call(
         functools.partial(gather_kernel, gx, gz),
-        in_specs=[pl.BlockSpec(memory_space=pl.ANY)] * 2,
-        out_specs=[pl.BlockSpec(memory_space=pl.ANY)] * 2,
+        in_specs=[pl.BlockSpec(memory_space=pltpu.VMEM)] * 2,
+        out_specs=[pl.BlockSpec(memory_space=pltpu.VMEM)] * 2,
         out_shape=[
             jax.ShapeDtypeStruct((gx,) + xs.shape, F32),
             jax.ShapeDtypeStruct((gz,) + zs.shape, F32),
@@ -406,7 +456,9 @@
         scratch_shapes=[
             dma((2,)), dma((gx - 1,)), dma((gx - 1,)), dma((gz - 1,)), dma((gz - 1,))
         ],
-        compiler_params=pltpu.CompilerParams(collective_id=1, has_side_effects=True),
+        compiler_params=pltpu.CompilerParams(
+            collective_id=1, has_side_effects=True, vmem_limit_bytes=8 * 1024 * 1024
+        ),
         name="gather_sums",
     )(xs, zs)
 
@@ -508,9 +560,9 @@
 
 
 def body(velocity):
-    ck, xup, xdn, zup, zdn = find_edges(velocity)
-    xl, xr, zl, zr = swap_edges(xup, xdn, zup, zdn)
-    grad_x, grad_z, convect, xs, zs = differentiate(velocity, ck, xl, xr, zl, zr)
+    ck, *edges = find_edges(velocity)
+    edges = swap_edges(*edges)
+    grad_x, grad_z, convect, xs, zs = differentiate(velocity, ck, *edges)
     xg, zg = gather_sums(xs, zs)
     rebuilt = rebuild(grad_x, grad_z, xg, zg)
     return grad_x, grad_z, convect, rebuilt

time: 101 us -> 84.5 us (0.84)
  local copies, waits for them, and re-layouts: 11.3 us -> 0.99 us
  Pallas kernels: 87.9 us -> 82.4 us
    unnamed x42 -> x14, local copies, waits for them, and re-layouts: 11.3 us -> 0.99 us
    pallas_call x1, Pallas kernels: 17.1 us -> 11.9 us  [swap_edges(): pl.pallas_call(functools.partial(neighbours_kernel, gx, gz), in_specs=[pl...]
    pallas_call x1, Pallas kernels: 36.3 us -> 34.5 us  [differentiate(): pl.pallas_call(functools.partial(main_kernel, steps), grid=(steps,), in_s...]
    pallas_call x1, Pallas kernels: 14.3 us -> 15.9 us  [find_edges(): pl.pallas_call(functools.partial(edges_kernel, steps), grid=(steps,), in_...]
where the time goes in v2:
time: 84.5 us; the launch traced here: 84.2 us
  Pallas kernels  82.4 us (98%)
  local copies, waits for them, and re-layouts  0.99 us (1%)
    pallas_call x1, Pallas kernels, differentiate(): pl.pallas_call(functools.partial(main_kernel, steps), grid=(steps,), in_s...  34.5 us
    pallas_call x1, Pallas kernels, find_edges(): pl.pallas_call(functools.partial(edges_kernel, steps), grid=(steps,), in_...  15.9 us
    pallas_call x1, Pallas kernels, swap_edges(): pl.pallas_call(functools.partial(neighbours_kernel, gx, gz), in_specs=[pl...  11.9 us
    pallas_call x1, Pallas kernels, rebuild(): pl.pallas_call(functools.partial(rebuild_kernel, cx * gx, cz * gz), grid=...  10.6 us
    pallas_call x1, Pallas kernels, gather_sums(): pl.pallas_call(functools.partial(gather_kernel, gx, gz), in_specs=[pl.Blo...  9.43 us

profile of v2, /device:TPU:0, one launch (start us, length us, event | category | flops | bytes accessed | tf_op | source)
XLA Modules:
  0.0 84.2 jit_solution(1458320128475338314)
XLA Ops:
  0.6 0.0 copy-start
  0.6 0.0 copy-start.1
  0.7 0.0 copy-start.3
  0.7 1.0 %copy-done.3 = f32[256,128]{1,0:T(8,128)S(1)} copy-done((f32[256,128]{1,0:T(8,128)S(1)}, f32[256,128]{1,0:T(8,128)}, u32[]{:S(2)}) %copy-start.3) | copy-done | bytes 131096
  1.7 0.0 copy-start.5
  1.7 0.0 copy-start.6
  1.7 0.0 copy-start.2
  1.7 0.0 copy-start.4
  1.7 15.9 %find_edges.1 = (f32[8,9,8,256]{3,2,1,0:T(8,128)S(1)}, f32[9,8,256]{2,1,0:T(8,128)S(1)}, f32[9,8,256]{2,1,0:T(8,128)S(1)}, f32[8,4096]{1,0:T(8,128)S(1)}, f32[8,...) custom-call(f32[3,512,8,256]{3,2,1,0:T(8,128)} %v_ref.3, f32[256,128]{1,0:T(8,128)S(1)} %copy-done.3), custom_call_target="tpu_custom_call" | custom-call | tf_op jit(solution)/shard_map/find_edges/pallas_call | solution.py:170
  17.6 11.9 %swap_edges.1 = (f32[9,8,256]{2,1,0:T(8,128)S(1)}, f32[9,8,256]{2,1,0:T(8,128)S(1)}, f32[8,4096]{1,0:T(8,128)S(1)}, f32[8,4096]{1,0:T(8,128)S(1)}, f32[8,4,128]{2,1,0:T(4,128)S(1)}, /*index=5*/f32[8,4,128]{2,1,0:T(4,128)S(1)}) custom-call(f32[9,8,256]{2,1,0:T(8,128)S(1)} %get-tuple-element.25.xup, f32[9,8,256]{2,1,0:T(8,128)S(1)} %get-tuple-element.26.xdn, ...), custom_call_target="tpu_custom_call" | custom-call | tf_op jit(solution)/shard_map/swap_edges/pallas_call | solution.py:244
  29.5 0.0 copy-done
  29.6 0.0 copy-done.1
  29.6 0.0 copy-done.5
  29.6 0.0 copy-done.6
  29.6 34.5 %differentiate.1 = (f32[3,512,8,256]{3,2,1,0:T(8,128)}, f32[3,512,8,256]{3,2,1,0:T(8,128)}, f32[3,512,8,256]{3,2,1,0:T(8,128)}, f32[2,8,256]{2,1,0:T(8,128)S(1)}, f32[8,8,128]{2,1,0:T(8,128)S(1)}) custom-call(f32[8]{0:T(128)S(1)} %copy-done.6, f32[3,512,8,256]{3,2,1,0:T(8,128)} %v_ref.3, f32[8,9,8,256]{3,2,1,0:T(8,128)S(1)} %get-tuple-element.24.ck_ref, ...), custom_call_target="tpu_custom_call" | custom-call | tf_op jit(solution)/shard_map/differentiate/pallas_call | solution.py:365
  64.1 9.4 %gather_sums.1 = (f32[4,2,8,256]{3,2,1,0:T(8,128)S(1)}, f32[8,8,8,128]{3,2,1,0:T(8,128)S(1)}) custom-call(f32[2,8,256]{2,1,0:T(8,128)S(1)} %get-tuple-element.40.xs, f32[8,8,128]{2,1,0:T(8,128)S(1)} %get-tuple-element.41.zs), custom_call_target="tpu_custom_call" | custom-call | tf_op jit(solution)/shard_map/gather_sums/pallas_call | solution.py:448
  73.6 0.0 copy-done.2
  73.6 0.0 copy-done.4
  73.6 10.6 %rebuild.1 = f32[2,512,8,256]{3,2,1,0:T(8,128)} custom-call(f32[4]{0:T(128)S(1)} %fusion.wx_ref, f32[8]{0:T(128)S(1)} %fusion.1.wz_ref, f32[4,2,8,256]{3,2,1,0:T(8,128)S(1)} %get-tuple-element.42.xg_ref, f32[8,8,8,128]{3,2,1,0:T(8,128)S(1)} %get-tuple-element.43.zg_ref, bf16[256,256]{1,0:T(8,128)(2,1)S(1)} %copy-done.2, bf16[128,256]{1,0:T(8,128)(2,1)S(1)} %copy-done.4, ...), custom_call_target="tpu_custom_call" | custom-call | tf_op jit(solution)/shard_map/rebuild/pallas_call | solution.py:535
  (2 shorter events, 0.0 us)
Async XLA Ops:
  0.6 28.9 %copy-start = (bf16[128,1536]{1,0:T(8,128)(2,1)S(1)}, bf16[128,1536]{1,0:T(8,128)(2,1)}, u32[]{:S(2)}) copy-start(bf16[128,1536]{1,0:T(8,128)(2,1)} %constant.45.clone.cm_ref) | copy-start | bytes 1179652
  0.6 28.9 %copy-start.1 = (bf16[768,256]{1,0:T(8,128)(2,1)S(1)}, bf16[768,256]{1,0:T(8,128)(2,1)}, u32[]{:S(2)}) copy-start(bf16[768,256]{1,0:T(8,128)(2,1)} %constant.44.clone.km_ref) | copy-start | bytes 1179652
  0.7 1.0 %copy-start.3 = (f32[256,128]{1,0:T(8,128)S(1)}, f32[256,128]{1,0:T(8,128)}, u32[]{:S(2)}) copy-start(f32[256,128]{1,0:T(8,128)} %constant.42.clone.w_ref) | copy-start | bytes 393220
  1.7 27.9 %copy-start.5 = (bf16[256,128]{1,0:T(8,128)(2,1)S(1)}, bf16[256,128]{1,0:T(8,128)(2,1)}, u32[]{:S(2)}) copy-start(bf16[256,128]{1,0:T(8,128)(2,1)} %constant.46.clone.sm_ref) | copy-start | bytes 196612
  1.7 27.9 %copy-start.6 = (f32[8]{0:T(128)S(1)}, f32[8]{0:T(128)}, u32[]{:S(2)}) copy-start(f32[8]{0:T(128)} %constant.43.clone.rp_ref) | copy-start | bytes 100
  1.7 71.9 %copy-start.2 = (bf16[256,256]{1,0:T(8,128)(2,1)S(1)}, bf16[256,256]{1,0:T(8,128)(2,1)}, u32[]{:S(2)}) copy-start(bf16[256,256]{1,0:T(8,128)(2,1)} %constant.47.clone.tm_ref) | copy-start | bytes 393220
  1.7 71.9 %copy-start.4 = (bf16[128,256]{1,0:T(8,128)(2,1)S(1)}, bf16[128,256]{1,0:T(8,128)(2,1)}, u32[]{:S(2)}) copy-start(bf16[128,256]{1,0:T(8,128)(2,1)} %constant.48.clone.pm_ref) | copy-start | bytes 196612

commit v3 on v2

--- a/solution.py
+++ b/solution.py
@@ -14,7 +14,8 @@
 C = 25.0 / 12.0
 KAPPA = -1.0 / 12.0
 TX = 64
-CHUNK = 16
+CHUNK = 32
+EDGE_CHUNK = 64
 STEP = 8
 F32 = jnp.float32
 BF16 = jnp.bfloat16
@@ -88,9 +89,9 @@
     return list(planes) + [planes[pivot] * p for p in planes]
 
 
-def chunk_operands(v_ref, begin):
+def chunk_operands(v_ref, begin, count):
     cz = v_ref.shape[3]
-    planes = [v_ref[c, pl.ds(begin, CHUNK)].reshape(CHUNK * 8, cz) for c in range(3)]
+    planes = [v_ref[c, pl.ds(begin, count)].reshape(count * 8, cz) for c in range(3)]
     return [split(value) for value in fields(planes, 2)]
 
 
@@ -115,25 +116,26 @@
     ck_ref[0] = back[...]
 
     def sweep(k, state):
-        begin = pl.multiple_of(TX - (k + 1) * CHUNK, CHUNK)
-        operands = chunk_operands(v_ref, begin)
+        begin = pl.multiple_of(TX - (k + 1) * EDGE_CHUNK, EDGE_CHUNK)
+        operands = chunk_operands(v_ref, begin, EDGE_CHUNK)
         joined = jnp.concatenate([part for pair in operands for part in pair], 1)
         turned = mm(joined, mat[...]).T
         message = turned[0:32] + turned[32:64]
-        at = pl.ds(pl.multiple_of(begin * 8, CHUNK * 8), CHUNK * 8)
+        at = pl.ds(pl.multiple_of(begin * 8, EDGE_CHUNK * 8), EDGE_CHUNK * 8)
         zup_ref[:, at] = message[0:8]
         zdn_ref[:, at] = message[16:24]
-        spot = pl.ds(TX // CHUNK - 1 - k, 1)
-        wup_ref[0, spot] = message[8:9]
-        wdn_ref[0, spot] = message[24:25]
+        for q in range(EDGE_CHUNK // 16):
+            spot = pl.ds(begin // 16 + q, 1)
+            wup_ref[0, spot] = message[8:9, 128 * q : 128 * q + 128]
+            wdn_ref[0, spot] = message[24:25, 128 * q : 128 * q + 128]
         states = list(state)
-        for j in range(CHUNK):
-            i = begin + (CHUNK - 1 - j)
+        for j in range(EDGE_CHUNK):
+            i = begin + (EDGE_CHUNK - 1 - j)
             now = fields([v_ref[c, i] for c in range(3)], 0)
             states = [ROOT * (f + b) for f, b in zip(now, states)]
         return tuple(states)
 
-    final = lax.fori_loop(0, TX // CHUNK, sweep, tuple(back[c] for c in range(6)))
+    final = lax.fori_loop(0, TX // EDGE_CHUNK, sweep, tuple(back[c] for c in range(6)))
     for c in range(6):
         back[c] = final[c]
     back[6:9] = v_ref[:, 0]
@@ -294,7 +296,7 @@
 
     def backward(k, state):
         begin = pl.multiple_of(TX - (k + 1) * CHUNK, CHUNK)
-        operands = chunk_operands(v_ref, begin)
+        operands = chunk_operands(v_ref, begin, CHUNK)
         joined = jnp.concatenate([jnp.concatenate([hi, hi, lo], 1) for hi, lo in operands], 0)
         slopes = mm(joined, km_ref[...])
         fixes = mm(msg[pl.ds(pl.multiple_of(begin * 8, CHUNK * 8), CHUNK * 8)], cm_ref[...])

time: 84.5 us -> 79.2 us (0.937)
  Pallas kernels: 82.4 us -> 77 us
    pallas_call x1, Pallas kernels: 15.9 us -> 12.2 us  [find_edges(): pl.pallas_call(functools.partial(edges_kernel, steps), grid=(steps,), in_...]
    pallas_call x1, Pallas kernels: 34.5 us -> 32.9 us  [differentiate(): pl.pallas_call(functools.partial(main_kernel, steps), grid=(steps,), in_s...]
where the time goes in v3:
time: 79.2 us; the launch traced here: 78.8 us
  Pallas kernels  77 us (97%)
  local copies, waits for them, and re-layouts  0.99 us (1%)
    pallas_call x1, Pallas kernels, differentiate(): pl.pallas_call(functools.partial(main_kernel, steps), grid=(steps,), in_s...  32.9 us
    pallas_call x1, Pallas kernels, find_edges(): pl.pallas_call(functools.partial(edges_kernel, steps), grid=(steps,), in_...  12.2 us
    pallas_call x1, Pallas kernels, swap_edges(): pl.pallas_call(functools.partial(neighbours_kernel, gx, gz), in_specs=[pl...  11.9 us
    pallas_call x1, Pallas kernels, rebuild(): pl.pallas_call(functools.partial(rebuild_kernel, cx * gx, cz * gz), grid=...  10.6 us
    pallas_call x1, Pallas kernels, gather_sums(): pl.pallas_call(functools.partial(gather_kernel, gx, gz), in_specs=[pl.Blo...  9.44 us

profile of v3, /device:TPU:0, one launch (start us, length us, event | category | flops | bytes accessed | tf_op | source)
XLA Modules:
  0.0 78.8 jit_solution(5047916970679389717)
XLA Ops:
  0.6 0.0 copy-start
  0.6 0.0 copy-start.1
  0.7 0.0 copy-start.3
  0.7 1.0 %copy-done.3 = f32[256,128]{1,0:T(8,128)S(1)} copy-done((f32[256,128]{1,0:T(8,128)S(1)}, f32[256,128]{1,0:T(8,128)}, u32[]{:S(2)}) %copy-start.3) | copy-done | bytes 131096
  1.7 0.0 copy-start.5
  1.7 0.0 copy-start.6
  1.7 0.0 copy-start.2
  1.7 0.0 copy-start.4
  1.7 12.2 %find_edges.1 = (f32[8,9,8,256]{3,2,1,0:T(8,128)S(1)}, f32[9,8,256]{2,1,0:T(8,128)S(1)}, f32[9,8,256]{2,1,0:T(8,128)S(1)}, f32[8,4096]{1,0:T(8,128)S(1)}, f32[8,...) custom-call(f32[3,512,8,256]{3,2,1,0:T(8,128)} %v_ref.3, f32[256,128]{1,0:T(8,128)S(1)} %copy-done.3), custom_call_target="tpu_custom_call" | custom-call | tf_op jit(solution)/shard_map/find_edges/pallas_call | solution.py:172
  13.8 11.9 %swap_edges.1 = (f32[9,8,256]{2,1,0:T(8,128)S(1)}, f32[9,8,256]{2,1,0:T(8,128)S(1)}, f32[8,4096]{1,0:T(8,128)S(1)}, f32[8,4096]{1,0:T(8,128)S(1)}, f32[8,4,128]{2,1,0:T(4,128)S(1)}, /*index=5*/f32[8,4,128]{2,1,0:T(4,128)S(1)}) custom-call(f32[9,8,256]{2,1,0:T(8,128)S(1)} %get-tuple-element.25.xup, f32[9,8,256]{2,1,0:T(8,128)S(1)} %get-tuple-element.26.xdn, ...), custom_call_target="tpu_custom_call" | custom-call | tf_op jit(solution)/shard_map/swap_edges/pallas_call | solution.py:246
  25.7 0.0 copy-done
  25.8 0.0 copy-done.1
  25.8 0.0 copy-done.5
  25.8 0.0 copy-done.6
  25.8 32.9 %differentiate.1 = (f32[3,512,8,256]{3,2,1,0:T(8,128)}, f32[3,512,8,256]{3,2,1,0:T(8,128)}, f32[3,512,8,256]{3,2,1,0:T(8,128)}, f32[2,8,256]{2,1,0:T(8,128)S(1)}, f32[8,8,128]{2,1,0:T(8,128)S(1)}) custom-call(f32[8]{0:T(128)S(1)} %copy-done.6, f32[3,512,8,256]{3,2,1,0:T(8,128)} %v_ref.3, f32[8,9,8,256]{3,2,1,0:T(8,128)S(1)} %get-tuple-element.24.ck_ref, ...), custom_call_target="tpu_custom_call" | custom-call | tf_op jit(solution)/shard_map/differentiate/pallas_call | solution.py:367
  58.7 9.4 %gather_sums.1 = (f32[4,2,8,256]{3,2,1,0:T(8,128)S(1)}, f32[8,8,8,128]{3,2,1,0:T(8,128)S(1)}) custom-call(f32[2,8,256]{2,1,0:T(8,128)S(1)} %get-tuple-element.40.xs, f32[8,8,128]{2,1,0:T(8,128)S(1)} %get-tuple-element.41.zs), custom_call_target="tpu_custom_call" | custom-call | tf_op jit(solution)/shard_map/gather_sums/pallas_call | solution.py:450
  68.2 0.0 copy-done.2
  68.2 0.0 copy-done.4
  68.2 10.6 %rebuild.1 = f32[2,512,8,256]{3,2,1,0:T(8,128)} custom-call(f32[4]{0:T(128)S(1)} %fusion.wx_ref, f32[8]{0:T(128)S(1)} %fusion.1.wz_ref, f32[4,2,8,256]{3,2,1,0:T(8,128)S(1)} %get-tuple-element.42.xg_ref, f32[8,8,8,128]{3,2,1,0:T(8,128)S(1)} %get-tuple-element.43.zg_ref, bf16[256,256]{1,0:T(8,128)(2,1)S(1)} %copy-done.2, bf16[128,256]{1,0:T(8,128)(2,1)S(1)} %copy-done.4, ...), custom_call_target="tpu_custom_call" | custom-call | tf_op jit(solution)/shard_map/rebuild/pallas_call | solution.py:537
  (2 shorter events, 0.0 us)
Async XLA Ops:
  0.6 25.1 %copy-start = (bf16[128,1536]{1,0:T(8,128)(2,1)S(1)}, bf16[128,1536]{1,0:T(8,128)(2,1)}, u32[]{:S(2)}) copy-start(bf16[128,1536]{1,0:T(8,128)(2,1)} %constant.45.clone.cm_ref) | copy-start | bytes 1179652
  0.6 25.1 %copy-start.1 = (bf16[768,256]{1,0:T(8,128)(2,1)S(1)}, bf16[768,256]{1,0:T(8,128)(2,1)}, u32[]{:S(2)}) copy-start(bf16[768,256]{1,0:T(8,128)(2,1)} %constant.44.clone.km_ref) | copy-start | bytes 1179652
  0.7 1.0 %copy-start.3 = (f32[256,128]{1,0:T(8,128)S(1)}, f32[256,128]{1,0:T(8,128)}, u32[]{:S(2)}) copy-start(f32[256,128]{1,0:T(8,128)} %constant.42.clone.w_ref) | copy-start | bytes 393220
  1.7 24.1 %copy-start.5 = (bf16[256,128]{1,0:T(8,128)(2,1)S(1)}, bf16[256,128]{1,0:T(8,128)(2,1)}, u32[]{:S(2)}) copy-start(bf16[256,128]{1,0:T(8,128)(2,1)} %constant.46.clone.sm_ref) | copy-start | bytes 196612
  1.7 24.1 %copy-start.6 = (f32[8]{0:T(128)S(1)}, f32[8]{0:T(128)}, u32[]{:S(2)}) copy-start(f32[8]{0:T(128)} %constant.43.clone.rp_ref) | copy-start | bytes 100
  1.7 66.5 %copy-start.2 = (bf16[256,256]{1,0:T(8,128)(2,1)S(1)}, bf16[256,256]{1,0:T(8,128)(2,1)}, u32[]{:S(2)}) copy-start(bf16[256,256]{1,0:T(8,128)(2,1)} %constant.47.clone.tm_ref) | copy-start | bytes 393220
  1.7 66.5 %copy-start.4 = (bf16[128,256]{1,0:T(8,128)(2,1)S(1)}, bf16[128,256]{1,0:T(8,128)(2,1)}, u32[]{:S(2)}) copy-start(bf16[128,256]{1,0:T(8,128)(2,1)} %constant.48.clone.pm_ref) | copy-start | bytes 196612

commit v4 on v3

--- a/solution.py
+++ b/solution.py
@@ -14,9 +14,9 @@
 C = 25.0 / 12.0
 KAPPA = -1.0 / 12.0
 TX = 64
-CHUNK = 32
+CHUNK = 64
 EDGE_CHUNK = 64
-STEP = 8
+STEP = 64
 F32 = jnp.float32
 BF16 = jnp.bfloat16
 LIMIT = 52 * 1024 * 1024

time: 79.2 us -> 77.2 us (0.975)
  Pallas kernels: 77 us -> 75 us
    pallas_call x1, Pallas kernels: 32.9 us -> 30.9 us  [differentiate(): pl.pallas_call(functools.partial(main_kernel, steps), grid=(steps,), in_s...]
where the time goes in v4:
time: 77.2 us; the launch traced here: 76.8 us
  Pallas kernels  75 us (97%)
  local copies, waits for them, and re-layouts  0.99 us (1%)
    pallas_call x1, Pallas kernels, differentiate(): pl.pallas_call(functools.partial(main_kernel, steps), grid=(steps,), in_s...  30.9 us
    pallas_call x1, Pallas kernels, find_edges(): pl.pallas_call(functools.partial(edges_kernel, steps), grid=(steps,), in_...  12.2 us
    pallas_call x1, Pallas kernels, swap_edges(): pl.pallas_call(functools.partial(neighbours_kernel, gx, gz), in_specs=[pl...  11.9 us
    pallas_call x1, Pallas kernels, rebuild(): pl.pallas_call(functools.partial(rebuild_kernel, cx * gx, cz * gz), grid=...  10.5 us
    pallas_call x1, Pallas kernels, gather_sums(): pl.pallas_call(functools.partial(gather_kernel, gx, gz), in_specs=[pl.Blo...  9.43 us

profile of v4, /device:TPU:0, one launch (start us, length us, event | category | flops | bytes accessed | tf_op | source)
XLA Modules:
  0.0 76.8 jit_solution(1186710401848938873)
XLA Ops:
  0.6 0.0 copy-start
  0.6 0.0 copy-start.1
  0.7 0.0 copy-start.3
  0.7 1.0 %copy-done.3 = f32[256,128]{1,0:T(8,128)S(1)} copy-done((f32[256,128]{1,0:T(8,128)S(1)}, f32[256,128]{1,0:T(8,128)}, u32[]{:S(2)}) %copy-start.3) | copy-done | bytes 131096
  1.7 0.0 copy-start.5
  1.7 0.0 copy-start.6
  1.7 0.0 copy-start.2
  1.7 0.0 copy-start.4
  1.7 12.2 %find_edges.1 = (f32[8,9,8,256]{3,2,1,0:T(8,128)S(1)}, f32[9,8,256]{2,1,0:T(8,128)S(1)}, f32[9,8,256]{2,1,0:T(8,128)S(1)}, f32[8,4096]{1,0:T(8,128)S(1)}, f32[8,...) custom-call(f32[3,512,8,256]{3,2,1,0:T(8,128)} %v_ref.3, f32[256,128]{1,0:T(8,128)S(1)} %copy-done.3), custom_call_target="tpu_custom_call" | custom-call | tf_op jit(solution)/shard_map/find_edges/pallas_call | solution.py:172
  13.9 11.9 %swap_edges.1 = (f32[9,8,256]{2,1,0:T(8,128)S(1)}, f32[9,8,256]{2,1,0:T(8,128)S(1)}, f32[8,4096]{1,0:T(8,128)S(1)}, f32[8,4096]{1,0:T(8,128)S(1)}, f32[8,4,128]{2,1,0:T(4,128)S(1)}, /*index=5*/f32[8,4,128]{2,1,0:T(4,128)S(1)}) custom-call(f32[9,8,256]{2,1,0:T(8,128)S(1)} %get-tuple-element.25.xup, f32[9,8,256]{2,1,0:T(8,128)S(1)} %get-tuple-element.26.xdn, ...), custom_call_target="tpu_custom_call" | custom-call | tf_op jit(solution)/shard_map/swap_edges/pallas_call | solution.py:246
  25.8 0.0 copy-done
  25.8 0.0 copy-done.1
  25.8 0.0 copy-done.5
  25.8 0.0 copy-done.6
  25.8 30.9 %differentiate.1 = (f32[3,512,8,256]{3,2,1,0:T(8,128)}, f32[3,512,8,256]{3,2,1,0:T(8,128)}, f32[3,512,8,256]{3,2,1,0:T(8,128)}, f32[2,8,256]{2,1,0:T(8,128)S(1)}, f32[8,8,128]{2,1,0:T(8,128)S(1)}) custom-call(f32[8]{0:T(128)S(1)} %copy-done.6, f32[3,512,8,256]{3,2,1,0:T(8,128)} %v_ref.3, f32[8,9,8,256]{3,2,1,0:T(8,128)S(1)} %get-tuple-element.24.ck_ref, ...), custom_call_target="tpu_custom_call" | custom-call | tf_op jit(solution)/shard_map/differentiate/pallas_call | solution.py:367
  56.8 9.4 %gather_sums.1 = (f32[4,2,8,256]{3,2,1,0:T(8,128)S(1)}, f32[8,8,8,128]{3,2,1,0:T(8,128)S(1)}) custom-call(f32[2,8,256]{2,1,0:T(8,128)S(1)} %get-tuple-element.40.xs, f32[8,8,128]{2,1,0:T(8,128)S(1)} %get-tuple-element.41.zs), custom_call_target="tpu_custom_call" | custom-call | tf_op jit(solution)/shard_map/gather_sums/pallas_call | solution.py:450
  66.2 0.0 copy-done.2
  66.2 0.0 copy-done.4
  66.2 10.5 %rebuild.1 = f32[2,512,8,256]{3,2,1,0:T(8,128)} custom-call(f32[4]{0:T(128)S(1)} %fusion.wx_ref, f32[8]{0:T(128)S(1)} %fusion.1.wz_ref, f32[4,2,8,256]{3,2,1,0:T(8,128)S(1)} %get-tuple-element.42.xg_ref, f32[8,8,8,128]{3,2,1,0:T(8,128)S(1)} %get-tuple-element.43.zg_ref, bf16[256,256]{1,0:T(8,128)(2,1)S(1)} %copy-done.2, bf16[128,256]{1,0:T(8,128)(2,1)S(1)} %copy-done.4, ...), custom_call_target="tpu_custom_call" | custom-call | tf_op jit(solution)/shard_map/rebuild/pallas_call | solution.py:537
  (2 shorter events, 0.0 us)
Async XLA Ops:
  0.6 25.2 %copy-start = (bf16[128,1536]{1,0:T(8,128)(2,1)S(1)}, bf16[128,1536]{1,0:T(8,128)(2,1)}, u32[]{:S(2)}) copy-start(bf16[128,1536]{1,0:T(8,128)(2,1)} %constant.45.clone.cm_ref) | copy-start | bytes 1179652
  0.6 25.2 %copy-start.1 = (bf16[768,256]{1,0:T(8,128)(2,1)S(1)}, bf16[768,256]{1,0:T(8,128)(2,1)}, u32[]{:S(2)}) copy-start(bf16[768,256]{1,0:T(8,128)(2,1)} %constant.44.clone.km_ref) | copy-start | bytes 1179652
  0.7 1.0 %copy-start.3 = (f32[256,128]{1,0:T(8,128)S(1)}, f32[256,128]{1,0:T(8,128)}, u32[]{:S(2)}) copy-start(f32[256,128]{1,0:T(8,128)} %constant.42.clone.w_ref) | copy-start | bytes 393220
  1.7 24.2 %copy-start.5 = (bf16[256,128]{1,0:T(8,128)(2,1)S(1)}, bf16[256,128]{1,0:T(8,128)(2,1)}, u32[]{:S(2)}) copy-start(bf16[256,128]{1,0:T(8,128)(2,1)} %constant.46.clone.sm_ref) | copy-start | bytes 196612
  1.7 24.2 %copy-start.6 = (f32[8]{0:T(128)S(1)}, f32[8]{0:T(128)}, u32[]{:S(2)}) copy-start(f32[8]{0:T(128)} %constant.43.clone.rp_ref) | copy-start | bytes 100
  1.7 64.6 %copy-start.2 = (bf16[256,256]{1,0:T(8,128)(2,1)S(1)}, bf16[256,256]{1,0:T(8,128)(2,1)}, u32[]{:S(2)}) copy-start(bf16[256,256]{1,0:T(8,128)(2,1)} %constant.47.clone.tm_ref) | copy-start | bytes 393220
  1.7 64.6 %copy-start.4 = (bf16[128,256]{1,0:T(8,128)(2,1)S(1)}, bf16[128,256]{1,0:T(8,128)(2,1)}, u32[]{:S(2)}) copy-start(bf16[128,256]{1,0:T(8,128)(2,1)} %constant.48.clone.pm_ref) | copy-start | bytes 196612
